TPU v7x, 32 devices: a whole 2x2x4 slice. The times are simulated.
32 devices in a mesh: space: 16 (over z, y, core), clus: 2 (over x).
Axes of the slice: x: 2, y: 2, z: 4, core: 2. Of those that a mesh axis runs over, the one named last changes fastest.
Arguments:
- features: bfloat16 [128, 128, 256], P('space', 'clus'), may hold values from -6 to 6
- weights: bfloat16 [16, 9, 256, 128], P('clus'), may hold values from -6 to 6
- tile_lists: int32 [16, 64], P('clus'), may hold values from 0 to 255, as said below
- labels: int32 [16, 64, 128], P('clus'), may hold values 0 or 1
Outputs:
- new_weights: bfloat16 [16, 9, 256, 128], P('clus', None, 'space')
Inputs may be any that keep to these rules, and one draw needn't show every extreme that they name: `tile_lists`: counting repeats, no list names more than 8 tiles t with the same t // 16, and some list names exactly 8. `tile_lists`: for every w and g, the entries 4 * w to 4 * w + 3 of the lists of clusters 8 * g to 8 * g + 7 name, counting repeats, at most 4 tiles t with the same t // 16, and exactly 4 for some value of t // 16.
All inputs are finite; a program needn't handle non-finite values. No bound on the sum of `labels` on one device may be relied on, other than what follows from the above.
Results may differ from a plain program's by a relative error of at most 0.0037.
Values may be sent and summed in bfloat16 or wider, within the bound.
A program may use at most 128 MiB of HBM per device.

v0:
```python
import math

import jax
import jax.numpy as jnp
from jax import lax
from jax.sharding import PartitionSpec as P


def padded_2(x, sides, width):
    for axis, dim in sides:
        size, length = (lax.axis_size(axis), x.shape[dim])
        up = [(i, (i + 1) % size) for i in range(size - 1)]
        down = [(j, i) for i, j in up]
        last = lax.slice_in_dim(x, length - width, length, axis=dim)
        initial = lax.slice_in_dim(x, 0, width, axis=dim)
        before = lax.ppermute(last, axis, up)
        after = lax.ppermute(initial, axis, down)
        x = jnp.concatenate([before, x, after], axis=dim)
    return x


def extended_tiles(features):
    gathered = lax.all_gather(features, "clus", axis=1, tiled=True)
    padded = padded_2(gathered, (("space", 0),), 1)
    side_cells = gathered.shape[0]
    tile_count = gathered.shape[1] // side_cells
    channels = gathered.shape[2]
    padded = jnp.pad(padded, ((0, 0), (1, side_cells), (0, 0)))
    main_cols = padded[:, : tile_count * side_cells].reshape(
        side_cells + 2, tile_count, side_cells, channels
    )
    tail_cols = padded[:, side_cells : side_cells + tile_count * side_cells].reshape(
        side_cells + 2, tile_count, side_cells, channels
    )[:, :, :2]
    joined = jnp.concatenate([main_cols, tail_cols], axis=2)
    return jnp.transpose(joined, (1, 0, 2, 3))


def head_gradient(tile_block, weights, target, live_slots):
    groups, depth = (tile_block.shape[0], tile_block.shape[1])
    side_cells = tile_block.shape[2] - 2
    channels = tile_block.shape[4]
    species = weights.shape[3]
    scaling = 1.0 / math.sqrt(9 * channels)
    rows_all = depth * side_cells * side_cells

    def window(tap_index):
        shift_row, shift_col = (tap_index // 3, tap_index % 3)
        return tile_block[
            :, :, shift_row : shift_row + side_cells, shift_col : shift_col + side_cells, :
        ].reshape(groups, rows_all, channels)

    logits = jnp.zeros((groups, rows_all, species), jnp.float32)
    for tap_index in range(9):
        logits = logits + jnp.einsum(
            "gnc,gcs->gns",
            window(tap_index),
            weights[:, tap_index],
            preferred_element_type=jnp.float32,
        )
    probability = jax.nn.sigmoid(logits * scaling).reshape(
        groups, depth, side_cells * side_cells, species
    )
    residual = (
        (probability - target[:, :, None, :])
        * live_slots[:, :, None, None]
        / (side_cells * side_cells)
    )
    residual = residual.astype(jnp.bfloat16).reshape(groups, rows_all, species)
    terms = jnp.stack(
        [
            scaling
            * jnp.einsum(
                "gnc,gns->gcs", window(tap_index), residual, preferred_element_type=jnp.float32
            )
            for tap_index in range(9)
        ],
        axis=1,
    )
    share = lax.psum_scatter(terms, "space", scatter_dimension=2, tiled=True)
    return share


def shards(features, weights, tile_lists, labels):
    extended = extended_tiles(features)
    tile_count = extended.shape[0]
    side_cells = extended.shape[1] - 2
    channels = weights.shape[2]
    list_length = tile_lists.shape[1]
    spaces = lax.axis_size("space")
    position = lax.axis_index("space")
    per_list = list_length // spaces
    depth = 2 * per_list
    owner_band = tile_lists // tile_count
    local_tile = tile_lists % tile_count
    owned_here = owner_band == position
    order_rank = jnp.cumsum(owned_here.astype(jnp.int32), axis=1) - 1
    slot_hits = owned_here[:, :, None] & (
        order_rank[:, :, None] == jnp.arange(depth, dtype=jnp.int32)[None, None, :]
    )
    slot_local = jnp.sum(jnp.where(slot_hits, local_tile[:, :, None], 0), axis=1)
    slot_weights = slot_hits.astype(jnp.float32)
    live_slots = jnp.sum(slot_weights, axis=1)
    target = jnp.einsum("glb,gls->gbs", slot_weights, labels.astype(jnp.float32))
    tile_block = jnp.take(extended, slot_local, axis=0)
    share = head_gradient(tile_block, weights, target, live_slots)
    step_rate = math.sqrt(9 * channels * side_cells * side_cells / list_length)
    share_rows = channels // spaces
    weight_share = lax.dynamic_slice_in_dim(weights, position * share_rows, share_rows, 2)
    return (weight_share.astype(jnp.float32) - step_rate * share).astype(jnp.bfloat16)


def solution(mesh):
    in_specs = (
        P("space", "clus", None),
        P("clus", None, None, None),
        P("clus", None),
        P("clus", None, None),
    )
    out_specs = P("clus", None, "space", None)
    return jax.shard_map(shards, mesh=mesh, in_specs=in_specs, out_specs=out_specs, check_vma=False)
```

profile of v0, /device:TPU:17, one launch (start us, length us, event | category | flops | bytes accessed | tf_op | source)
XLA Modules:
  0.0 214.9 jit_solution(10664131604596926297)
XLA Ops:
  6.5 0.0 reduce-scatter.2.cloned.1.call-start
  6.5 8.0 %all_gather.3 = bf16[8,128,256]{2,1,0:T(8,128)(2,1)S(1)} all-gather(bf16[8,64,256]{2,1,0:T(8,128)(2,1)} %param.4), channel_id=1, replica_groups=mesh['space'=16,'clus'=2] {'clus'}, dimensions={1}, use_global_device_ids=true | all-gather | bytes 786432 | tf_op jit(solution)/shard_map/all_gather | solution.py:23
  14.6 4.6 %collective-permute-start = (bf16[1,128,256]{2,1,0:T(8,128)(2,1)S(1)}, bf16[1,128,256]{2,1,0:T(8,128)(2,1)S(1)}, u32[]{:S(2)}, u32[]{:S(2)}) collective-permute-start(bf16[1,128,256]{2,1,0:T(8,128)(2,1)S(1)} %get-tuple-element.18), channel_id=1, source_target_pairs={{0,2},{2,4},{4,6},{6,8},{8,10},{10,12},{12,14},{14,16},{16,18},{18... | collective-permute-start | bytes 196616 | tf_op jit(solution)/shard_map/ppermute | solution.py:16
  19.2 1.9 collective-permute-start.1
  21.1 0.7 fusion.62
  21.8 0.2 reduce_window_sum.11
  22.0 0.7 add_select_fusion
  22.7 0.2 select_reduce_fusion
  23.0 0.1 convert_reduce_fusion
  23.1 0.1 reshape.88
  23.1 1.1 fusion.53
  24.2 0.1 mul.58
  24.3 0.1 mul.59
  24.4 0.0 collective-permute-done
  24.4 0.4 collective-permute-done.1
  24.8 0.2 fusion.26
  25.0 0.1 slice_bitcast_fusion.1
  25.1 0.1 slice.107
  25.2 0.2 maximum_bitcast_fusion
  25.4 3.3 %gather_fusion = bf16[64,10,10,256]{3,2,1,0:T(8,128)(2,1)} fusion(bf16[16,10,10,256]{3,2,0,1:T(8,128)(2,1)S(1)} %maximum_bitcast_fusion, s32[1024]{0:T(1024)S(1)} %pad_clamp_fusion), kind=kCustom, calls=%fused_computation | custom fusion | bytes 6553856 | tf_op jit(solution)/shard_map/jit(_take)/gather | solution.py:105
  28.7 5.3 %broadcast_select_fusion = bf16[8,8,10,10,256]{4,3,2,1,0:T(8,128)(2,1)} fusion(bf16[8,8,10,10,256]{4,3,2,1,0:T(8,128)(2,1)} %bitcast.136, pred[8,8]{1,0:T(8,128)(4,1)S(1)} %compare_and_fusion), kind=kLoop, calls=%fused_computation.1 | loop fusion | flops 1638400 | bytes 6553664 | tf_op jit(solution)/shard_map/jit(_take)/select_n | solution.py:105
  34.0 17.7 %fusion.64 = (bf16[8,8,8,8,256]{4,3,2,1,0:T(8,128)(2,1)S(1)}, bf16[8,8,8,8,256]{4,3,2,1,0:T(8,128)(2,1)}, bf16[8,8,8,8,256]{4,3,2,1,0:T(8,128)(2,1)}, bf16[8,8,8...) fusion(bf16[8,8,10,10,256]{4,3,2,1,0:T(8,128)(2,1)} %broadcast_, ...), kind=kLoop, calls=%fused_computation.95 | loop fusion | bytes 37748736 | tf_op jit(solution)/shard_map/slice | solution.py:49
  51.7 0.0 copy-start.1
  51.7 2.5 %fusion.28 = f32[8,512,128]{2,1,0:T(8,128)S(1)} fusion(bf16[8,512,256]{2,1,0:T(8,128)(2,1)} %bitcast.139, bf16[8,9,256,128]{3,2,1,0:T(8,128)(2,1)} %param.5), kind=kOutput, calls=%fused_computation.46 | convolution fusion | flops 268435456 | bytes 4718592 | tf_op jit(solution)/shard_map/gnc,gcs->gns/dot_general | solution.py:55
  54.2 0.0 copy-done.1
  54.2 0.0 copy-start.2
  54.3 1.9 fusion.30
  56.2 0.0 copy-done.2
  56.2 0.0 copy-start.3
  56.2 1.9 fusion.32
  58.1 0.0 copy-done.3
  58.1 0.0 copy-start.4
  58.1 1.9 fusion.34
  60.0 0.0 copy-done.4
  60.0 0.0 copy-start.5
  60.0 3.3 %fusion.36 = f32[8,512,128]{2,1,0:T(8,128)} fusion(bf16[8,512,256]{2,1,0:T(8,128)(2,1)S(1)} %bitcast.147, bf16[8,9,256,128]{3,2,1,0:T(8,128)(2,1)} %param.5), kind=kOutput, calls=%fused_computation.54 | convolution fusion | flops 268435456 | bytes 4718592 | tf_op jit(solution)/shard_map/gnc,gcs->gns/dot_general | solution.py:55
  63.3 0.0 copy-done.5
  63.3 0.0 copy-start.6
  63.3 3.2 %fusion.38 = f32[8,512,128]{2,1,0:T(8,128)} fusion(bf16[8,512,256]{2,1,0:T(8,128)(2,1)S(1)} %bitcast.149, bf16[8,9,256,128]{3,2,1,0:T(8,128)(2,1)} %param.5), kind=kOutput, calls=%fused_computation.56 | convolution fusion | flops 268435456 | bytes 4718592 | tf_op jit(solution)/shard_map/gnc,gcs->gns/dot_general | solution.py:55
  66.5 0.0 copy-done.6
  66.5 0.0 copy-start.7
  66.5 3.3 %fusion.40 = f32[8,512,128]{2,1,0:T(8,128)} fusion(bf16[8,512,256]{2,1,0:T(8,128)(2,1)S(1)} %bitcast.151, bf16[8,9,256,128]{3,2,1,0:T(8,128)(2,1)} %param.5), kind=kOutput, calls=%fused_computation.58 | convolution fusion | flops 268435456 | bytes 4718592 | tf_op jit(solution)/shard_map/gnc,gcs->gns/dot_general | solution.py:55
  69.8 0.0 copy-done.7
  69.8 3.1 %fusion.42 = f32[8,512,128]{2,1,0:T(8,128)} fusion(bf16[8,512,256]{2,1,0:T(8,128)(2,1)S(1)} %bitcast.153, bf16[8,9,256,128]{3,2,1,0:T(8,128)(2,1)} %param.5), kind=kOutput, calls=%fused_computation.60 | convolution fusion | flops 268435456 | bytes 4718592 | tf_op jit(solution)/shard_map/gnc,gcs->gns/dot_general | solution.py:55
  72.9 4.9 %fusion.2 = bf16[8,512,128]{2,1,0:T(8,128)(2,1)S(1)} fusion(f32[8,512,128]{2,1,0:T(8,128)S(1)} %fusion.28, f32[8,512,128]{2,1,0:T(8,128)S(1)} %fusion.30, f32[8,512,128]{2,1,0:T(8,128)S(1)} %fusion.32, f32[8,512,128]{2,1,0:T(8,128)S(1)} %fusion.34, f32[8,512,128]{2,1,0:T(8,128)} %fusion.36, f32[8,512,128]{2,1,0:T(8,128)} %fusion.38, ...), kind=kOutput, calls=%fused_computation.7 | convolution fusion | flops 276824064 | bytes 20496384 | tf_op jit(solution)/shard_map/gnc,gcs->gns/dot_general | solution.py:55
  77.8 1.8 fusion.21
  79.5 1.8 fusion.19
  81.4 1.8 fusion.17
  83.2 1.8 fusion.15
  85.0 1.8 fusion.13
  86.8 1.8 fusion.11
  88.6 0.0 copy-start
  88.6 1.8 fusion.9
  90.4 0.0 copy-done
  90.4 1.8 fusion.7
  92.2 1.9 fusion.5
  94.1 0.0 reduce-scatter.2.cloned.1.call-update
  94.1 112.0 %reduce-scatter.2.cloned.1.call-done = f32[8,9,16,128]{3,2,0,1:T(8,128)} async-done(((f32[8,9,256,128]{3,2,0,1:T(8,128)}), f32[8,9,16,128]{3,2,0,1:T(8,128)}) %reduce-scatter.2.cloned.1.call-update) | async-done | bytes 589840 | tf_op jit(solution)/shard_map/reduce_scatter | solution.py:80
  206.1 1.2 subtract_convert_fusion
  207.3 0.7 copy.24
  (4 shorter events, 0.0 us)
Async XLA Ops:
  6.5 199.6 %reduce-scatter.2.cloned.1.call-start = ((), (), s32[]{:S(2)}) async-start(), calls=%async_computation.1 | async-start | bytes 10027008 | tf_op jit(solution)/shard_map/reduce_scatter | solution.py:80
  14.6 9.8 %collective-permute-start = (bf16[1,128,256]{2,1,0:T(8,128)(2,1)S(1)}, bf16[1,128,256]{2,1,0:T(8,128)(2,1)S(1)}, u32[]{:S(2)}, u32[]{:S(2)}) collective-permute-start(bf16[1,128,256]{2,1,0:T(8,128)(2,1)S(1)} %get-tuple-element.18), channel_id=1, source_target_pairs={{0,2},{2,4},{4,6},{6,8},{8,10},{10,12},{12,14},{14,16},{16,18},{18... | collective-permute-start | bytes 196616 | tf_op jit(solution)/shard_map/ppermute | solution.py:16
  19.2 5.6 %collective-permute-start.1 = (bf16[1,128,256]{2,1,0:T(8,128)(2,1)S(1)}, bf16[1,128,256]{2,1,0:T(8,128)(2,1)S(1)}, u32[]{:S(2)}, u32[]{:S(2)}) collective-permute-start(bf16[1,128,256]{2,1,0:T(8,128)(2,1)S(1)} %get-tuple-element.19), channel_id=1, source_target_pairs={{2,0},{4,2},{6,4},{8,6},{10,8},{12,10},{14,12},{16,14},{18,16},{20... | collective-permute-start | bytes 196616 | tf_op jit(solution)/shard_map/ppermute | solution.py:17
  51.7 2.5 %copy-start.1 = (bf16[8,8,8,8,256]{4,3,2,1,0:T(8,128)(2,1)S(1)}, bf16[8,8,8,8,256]{4,3,2,1,0:T(8,128)(2,1)}, u32[]{:S(2)}) copy-start(bf16[8,8,8,8,256]{4,3,2,1,0:T(8,128)(2,1)} %get-tuple-element.9) | copy-start | bytes 6291460
  54.2 1.9 copy-start.2
  56.2 1.9 copy-start.3
  58.1 1.9 copy-start.4
  60.0 3.3 %copy-start.5 = (bf16[8,8,8,8,256]{4,3,2,1,0:T(8,128)(2,1)S(1)}, bf16[8,8,8,8,256]{4,3,2,1,0:T(8,128)(2,1)}, u32[]{:S(2)}) copy-start(bf16[8,8,8,8,256]{4,3,2,1,0:T(8,128)(2,1)} %get-tuple-element.13) | copy-start | bytes 6291460
  63.3 3.2 %copy-start.6 = (bf16[8,8,8,8,256]{4,3,2,1,0:T(8,128)(2,1)S(1)}, bf16[8,8,8,8,256]{4,3,2,1,0:T(8,128)(2,1)}, u32[]{:S(2)}) copy-start(bf16[8,8,8,8,256]{4,3,2,1,0:T(8,128)(2,1)} %get-tuple-element.14) | copy-start | bytes 6291460
  66.5 3.3 %copy-start.7 = (bf16[8,8,8,8,256]{4,3,2,1,0:T(8,128)(2,1)S(1)}, bf16[8,8,8,8,256]{4,3,2,1,0:T(8,128)(2,1)}, u32[]{:S(2)}) copy-start(bf16[8,8,8,8,256]{4,3,2,1,0:T(8,128)(2,1)} %get-tuple-element.15) | copy-start | bytes 6291460
  88.6 1.8 copy-start
Sparse Core Ops, SparseCore 0:
  94.2 111.8 reduce-scatter.1
where the time goes:
time: 217 us; the launch traced here: 215 us
  waiting for transfers between devices  112 us (52%)
  matrix products  43.3 us (20%)
  local copies, waits for them, and re-layouts  22.2 us (10%)
  between operations  13.6 us (6%)
  other arithmetic  8.89 us (4%)
  blocking collectives  8.05 us (4%)
  starting transfers between devices  6.5 us (3%)
    reduce_scatter x1, waiting for transfers between devices, head_gradient(): share = lax.psum_scatter(terms, 'space', scatter_dimension=2, tiled=True)  112 us
    dot_general x9, matrix products, head_gradient(): jnp.einsum('gnc,gcs->gns', window(tap_index), weights[:, tap_index], pref...  25.9 us
    slice x1, local copies, waits for them, and re-layouts, window(): tile_block[:, :, shift_row:shift_row + side_cells, shift_col:shift_col +...  17.7 us
    dot_general x9, matrix products, head_gradient(): jnp.einsum('gnc,gns->gcs', window(tap_index), residual, preferred_element...  16.3 us
    all_gather x1, blocking collectives, extended_tiles(): gathered = lax.all_gather(features, 'clus', axis=1, tiled=True)  8.05 us
    select_n x2, other arithmetic, shards(): tile_block = jnp.take(extended, slot_local, axis=0)  5.33 us
    ppermute x1, starting transfers between devices, padded_2(): before = lax.ppermute(last, axis, up)  4.58 us
  transfers between devices with their start and end apart: 3, of which 2 were waited for; matrix products, arithmetic and copies ran while one was open for 2% of the time, Pallas kernels for 0%

commit v1 on v0

v1 whole, which is shorter than its diff:
```python
import functools
import math

import jax
import jax.numpy as jnp
from jax import lax
from jax.experimental import pallas as pl
from jax.experimental.pallas import tpu as pltpu
from jax.sharding import PartitionSpec as P

SIDE = 8
BATCH = 4


def head_kernel(group_ref, lists_ref, map_ref, weights_ref, labels_ref, grad_ref, wide, cols, acc, chosen):
    clusters, length = lists_ref.shape
    rows_all, columns, channels = map_ref.shape
    tiles = columns // SIDE
    bands = (rows_all - 2) // SIDE
    per_group = tiles * bands
    species = weights_ref.shape[2]
    group = group_ref[0]
    scaling = 1.0 / math.sqrt(9 * channels)
    cells = SIDE * SIDE

    def widen(row, carry):
        wide[row, 1 : tiles + 1] = map_ref[row].astype(jnp.float32).reshape(tiles, SIDE, channels)
        wide[row, 0] = jnp.zeros((SIDE, channels), jnp.float32)
        wide[row, tiles + 1] = jnp.zeros((SIDE, channels), jnp.float32)
        return carry

    lax.fori_loop(0, rows_all, widen, 0)
    side_row = lax.broadcasted_iota(jnp.int32, (SIDE + 2, SIDE, channels), 1)

    def one_cluster(c, carry):
        def choose(k, count):
            chosen[count] = k
            return count + (lists_ref[c, k] // per_group == group).astype(jnp.int32)

        count = lax.fori_loop(0, length, choose, jnp.int32(0))
        acc[...] = jnp.zeros_like(acc)

        def one_batch(b, carry):
            targets = []
            for j in range(BATCH):
                slot = b * BATCH + j
                k = chosen[jnp.minimum(slot, count - 1)]
                tile = lists_ref[c, k] - group * per_group
                band, column = tile // tiles, tile % tiles
                rows = pl.ds(band * SIDE, SIDE + 2)
                left, mid, right = wide[rows, column], wide[rows, column + 1], wide[rows, column + 2]
                shifted = (
                    jnp.where(side_row == 0, pltpu.roll(left, 1, 1), pltpu.roll(mid, 1, 1)),
                    mid,
                    jnp.where(
                        side_row == SIDE - 1,
                        pltpu.roll(right, SIDE - 1, 1),
                        pltpu.roll(mid, SIDE - 1, 1),
                    ),
                )
                for dx in range(3):
                    flat = shifted[dx].reshape((SIDE + 2) * SIDE, channels)
                    for dy in range(3):
                        tap = 3 * dy + dx
                        cols[j * cells : (j + 1) * cells, tap * channels : (tap + 1) * channels] = flat[
                            dy * SIDE : dy * SIDE + cells
                        ].astype(jnp.bfloat16)
                targets.append(jnp.broadcast_to(labels_ref[c, k].astype(jnp.float32), (cells, species)))
            target = jnp.concatenate(targets, axis=0)
            logits = jnp.dot(cols[...], weights_ref[c], preferred_element_type=jnp.float32)
            probability = jax.nn.sigmoid(logits * scaling)
            slots = b * BATCH + lax.broadcasted_iota(jnp.int32, (BATCH * cells, species), 0) // cells
            residual = jnp.where(slots < count, (probability - target) * (1.0 / cells), 0.0)
            residual = residual.astype(jnp.bfloat16)
            acc[...] += lax.dot_general(
                residual, cols[...], (((0,), (0,)), ((), ())), preferred_element_type=jnp.float32
            )
            return carry

        lax.fori_loop(0, (count + BATCH - 1) // BATCH, one_batch, 0)
        for tap in range(9):
            part = slice(tap * channels, (tap + 1) * channels)
            grad_ref[c, part, :] = acc[:, part].T.astype(grad_ref.dtype)
        return carry

    lax.fori_loop(0, clusters, one_cluster, 0)


def gradient_shares(group, lists, rows, weights, labels):
    clusters, taps, channels, species = weights.shape
    rows_all, columns, _ = rows.shape
    smem = pl.BlockSpec(memory_space=pltpu.SMEM)
    vmem = pl.BlockSpec(memory_space=pltpu.VMEM)
    return pl.pallas_call(
        head_kernel,
        out_shape=jax.ShapeDtypeStruct((clusters, taps * channels, species), jnp.bfloat16),
        in_specs=[smem, smem, vmem, vmem, vmem],
        out_specs=vmem,
        scratch_shapes=[
            pltpu.VMEM((rows_all, columns // SIDE + 2, SIDE, channels), jnp.float32),
            pltpu.VMEM((BATCH * SIDE * SIDE, taps * channels), jnp.bfloat16),
            pltpu.VMEM((species, taps * channels), jnp.float32),
            pltpu.SMEM((lists.shape[1],), jnp.int32),
        ],
        compiler_params=pltpu.CompilerParams(vmem_limit_bytes=40 * 2**20),
        cost_estimate=pl.CostEstimate(flops=5 * 10**9, bytes_accessed=6 * 10**6, transcendentals=0),
    )(
        group.reshape(1),
        lists,
        rows,
        weights.reshape(clusters, taps * channels, species),
        labels.reshape(clusters, labels.shape[1], 1, species),
    )


def shards(members, features, weights, tile_lists, labels):
    spaces = lax.axis_size("space")
    position = lax.axis_index("space")
    groups = spaces // members
    group, member = position // members, position % members
    inner = [[g * members + j for j in range(members)] for g in range(groups)]
    outer = [[g * members + j for g in range(groups)] for j in range(members)]
    clusters, taps, channels, species = weights.shape
    mine = clusters // members

    rows = lax.all_gather(features, "clus", axis=1, tiled=True)
    rows = lax.all_gather(rows, "space", axis=0, tiled=True, axis_index_groups=inner)
    up = [(i, i + members) for i in range(spaces - members)]
    down = [(j, i) for i, j in up]
    before = lax.ppermute(rows[-1:], "space", up)
    after = lax.ppermute(rows[:1], "space", down)
    rows = jnp.concatenate([before, rows, after], axis=0)

    own = lambda x: lax.dynamic_slice_in_dim(x, member * mine, mine, 0)
    own_weights = own(weights)
    share = gradient_shares(group, own(tile_lists), rows, own_weights, own(labels))
    share = share.reshape(mine, taps, channels, species)
    total = lax.psum_scatter(
        share, "space", scatter_dimension=2, axis_index_groups=outer, tiled=True
    ).astype(jnp.float32)
    step = math.sqrt(9 * channels * SIDE * SIDE / tile_lists.shape[1]) / math.sqrt(9 * channels)
    depth = channels // groups
    old = lax.dynamic_slice_in_dim(own_weights, group * depth, depth, 2).astype(jnp.float32)
    new = (old - step * total).astype(jnp.bfloat16)
    return lax.all_to_all(
        new, "space", split_axis=2, concat_axis=0, axis_index_groups=inner, tiled=True
    )


def solution(mesh):
    in_specs = (
        P("space", "clus", None),
        P("clus", None, None, None),
        P("clus", None),
        P("clus", None, None),
    )
    out_specs = P("clus", None, "space", None)
    members = math.gcd(4, mesh.shape["space"])
    return jax.shard_map(
        functools.partial(shards, members),
        mesh=mesh,
        in_specs=in_specs,
        out_specs=out_specs,
        check_vma=False,
    )
```

time: 217 us -> 133 us (0.61)
  the two profiles are of different devices: /device:TPU:17 before, /device:TPU:0 now
where the time goes in v1:
time: 133 us
  waiting for transfers between devices  69.2 us (52%)
  blocking collectives  23.4 us (18%)
  between operations  13.5 us (10%)
  Pallas kernels  10.4 us (8%)
  local copies, waits for them, and re-layouts  7.09 us (5%)
  starting transfers between devices  5.89 us (4%)
  other arithmetic  3.17 us (2%)
    reduce_scatter x1, waiting for transfers between devices, shards(): lax.psum_scatter(share, 'space', scatter_dimension=2, axis_index_groups=o...  46.4 us
    all_gather x1, waiting for transfers between devices, shards(): lax.all_gather(rows, 'space', axis=0, tiled=True, axis_index_groups=inner)  21.6 us
    all_gather x1, blocking collectives, shards(): rows = lax.all_gather(features, 'clus', axis=1, tiled=True)  12 us
    all_to_all x1, blocking collectives, shards(): lax.all_to_all(new, 'space', split_axis=2, concat_axis=0, axis_index_grou...  11.4 us
    pallas_call x1, Pallas kernels, gradient_shares(): pl.pallas_call(head_kernel, out_shape=jax.ShapeDtypeStruct((clusters, tap...  10.4 us
    ppermute x1, starting transfers between devices, shards(): before = lax.ppermute(rows[-1:], 'space', up)  4.55 us
  transfers between devices with their start and end apart: 4, of which 3 were waited for; matrix products, arithmetic and copies ran while one was open for 2% of the time, Pallas kernels for 0%

profile of v1, /device:TPU:0, one launch (start us, length us, event | category | flops | bytes accessed | tf_op | source)
XLA Modules:
  0.0 132.6 jit_solution(4047709147227632953)
XLA Ops:
  6.5 0.0 copy-start
  6.5 0.0 all-gather.2.cloned.1.call-start
  6.5 12.0 %all_gather.6 = bf16[8,128,256]{2,1,0:T(8,128)(2,1)} all-gather(bf16[8,64,256]{2,1,0:T(8,128)(2,1)} %param.4), channel_id=1, replica_groups=mesh['space'=16,'clus'=2] {'clus'}, dimensions={1}, use_global_device_ids=true | all-gather | bytes 786432 | tf_op jit(solution)/shard_map/all_gather | solution.py:126
  18.5 0.0 all-gather.2.cloned.1.call-update
  18.6 0.0 reduce-scatter.2.cloned.1.call-start
  18.6 0.0 copy-done
  18.7 1.4 %constant_dynamic-slice_fusion.1 = bf16[2,9,256,128]{3,2,1,0:T(8,128)(2,1)S(1)} fusion(bf16[8,9,256,128]{3,2,1,0:T(8,128)(2,1)} %param.5, s32[]{:T(128)S(6)} %select_n.24), kind=kLoop, calls=%fused_computation.3 | loop fusion | bytes 2359300 | tf_op jit(solution)/shard_map/dynamic_slice | solution.py:134
  20.0 21.6 %all-gather.2.cloned.1.call-done = bf16[32,128,256]{2,1,0:T(8,128)(2,1)} async-done(((bf16[8,128,256]{2,1,0:T(8,128)(2,1)}), bf16[32,128,256]{2,1,0:T(8,128)(2,1)}) %all-gather.2.cloned.1.call-update) | async-done | bytes 2097168 | tf_op jit(solution)/shard_map/all_gather | solution.py:127
  41.6 0.9 fusion
  42.5 1.3 collective-permute-start.1
  43.8 4.5 %collective-permute-start = (bf16[1,128,256]{2,1,0:T(8,128)(2,1)S(1)}, bf16[1,128,256]{2,1,0:T(8,128)(2,1)S(1)}, u32[]{:S(2)}, u32[]{:S(2)}) collective-permute-start(bf16[1,128,256]{2,1,0:T(8,128)(2,1)S(1)} %get-tuple-element.5), channel_id=1, source_target_pairs={{0,8},{2,10},{4,12},{6,14},{8,16},{10,18},{12,20},{14,22},{16,24},... | collective-permute-start | bytes 196616 | tf_op jit(solution)/shard_map/ppermute | solution.py:130
  48.4 0.7 constant_dynamic-slice_fusion.2.lists_ref
  49.1 0.0 collective-permute-done.1
  49.1 1.2 collective-permute-done
  50.3 1.9 %pad_maximum_fusion.map_ref = bf16[34,128,256]{2,1,0:T(8,128)(2,1)S(1)} fusion(bf16[1,128,256]{2,1,0:T(8,128)(2,1)S(1)} %collective-permute-done.1, bf16[32,128,256]{2,1,0:T(8,128)(2,1)} %all-gather.2.cloned.1.call-done, bf16[1,128,256]{2,1,0:T(8,128)(2,1)S(1)} %collective-permute-done), kind=kLoop, calls=%fused_computation | loop fusion | flops 2228224 | bytes 4456448 | tf_op jit(solution)/shard_map/concatenate | solution.py:132
  52.1 10.4 %shard_map.46 = bf16[2,2304,128]{2,1,0:T(8,128)(2,1)S(1)} custom-call(s32[1]{0:T(128)} %bitcast.group_ref, s32[2,64]{1,0:T(2,128)S(1)} %constant_dynamic-slice_fusion.2.lists_ref, bf16[34,128,256]{2,1,0:T(8,128)(2,1)S(1)} %pad_maximum_fusion.map_ref, bf16[2,2304,128]{2,1,0:T(8,128)(2,1)S(1)} %bitcast.9, s32[2,64,1,128]{3,2,1,0:T(1,128)S(1)} %bitcast.10), custom_call_target="tpu_custom_call" | custom-call | flops 5000000000 | bytes 6000000 | tf_op jit(solution)/shard_map/pallas_call | solution.py:94
  62.5 2.2 %copy.7 = bf16[2,9,256,128]{3,1,0,2:T(8,128)(2,1)} copy(bf16[2,9,256,128]{3,2,1,0:T(8,128)(2,1)S(1)} %bitcast.8) | data formatting | bytes 2359296 | tf_op jit(solution)/shard_map/reshape | solution.py:137
  64.8 0.0 reduce-scatter.2.cloned.1.call-update
  64.8 1.1 constant_dynamic-slice_fusion.3
  65.9 46.4 %reduce-scatter.2.cloned.1.call-done = bf16[2,9,64,128]{3,1,0,2:T(8,128)(2,1)} async-done(((bf16[2,9,256,128]{3,1,0,2:T(8,128)(2,1)}), bf16[2,9,64,128]{3,1,0,2:T(8,128)(2,1)}) %reduce-scatter.2.cloned.1.call-update) | async-done | bytes 294928 | tf_op jit(solution)/shard_map/reduce_scatter | solution.py:138
  112.3 1.3 subtract_convert_fusion
  113.5 11.4 %all_to_all.18 = bf16[2,9,64,128]{3,1,0,2:T(8,128)(2,1)S(1)} all-to-all(bf16[2,9,64,128]{3,1,0,2:T(8,128)(2,1)S(1)} %subtract_convert_fusion), channel_id=1, replica_groups={{0,2,4,6},{8,10,12,14},{16,18,20,22},{24,26,28,30},{1,3,5,7},{9,11,13,1..., dimensions={2} | all-to-all | bytes 589824 | tf_op jit(solution)/shard_map/all_to_all | solution.py:145
  124.9 0.8 copy.8
  (1 shorter events, 0.0 us)
Async XLA Ops:
  6.5 12.1 %copy-start = (s32[8,64,128]{2,1,0:T(8,128)S(1)}, s32[8,64,128]{2,1,0:T(8,128)}, u32[]{:S(2)}) copy-start(s32[8,64,128]{2,1,0:T(8,128)} %param.7) | copy-start | bytes 786436
  6.5 35.1 %all-gather.2.cloned.1.call-start = ((), (), s32[]{:S(2)}) async-start(), calls=%async_computation.2 | async-start | bytes 2621440 | tf_op jit(solution)/shard_map/all_gather | solution.py:127
  18.6 93.7 %reduce-scatter.2.cloned.1.call-start = ((), (), s32[]{:S(2)}) async-start(), calls=%async_computation.3 | async-start | bytes 2621440 | tf_op jit(solution)/shard_map/reduce_scatter | solution.py:138
  42.5 6.6 %collective-permute-start.1 = (bf16[1,128,256]{2,1,0:T(8,128)(2,1)S(1)}, bf16[1,128,256]{2,1,0:T(8,128)(2,1)S(1)}, u32[]{:S(2)}, u32[]{:S(2)}) collective-permute-start(bf16[1,128,256]{2,1,0:T(8,128)(2,1)S(1)} %get-tuple-element.6), channel_id=1, source_target_pairs={{8,0},{10,2},{12,4},{14,6},{16,8},{18,10},{20,12},{22,14},{24,16},... | collective-permute-start | bytes 196616 | tf_op jit(solution)/shard_map/ppermute | solution.py:131
  43.8 6.4 %collective-permute-start = (bf16[1,128,256]{2,1,0:T(8,128)(2,1)S(1)}, bf16[1,128,256]{2,1,0:T(8,128)(2,1)S(1)}, u32[]{:S(2)}, u32[]{:S(2)}) collective-permute-start(bf16[1,128,256]{2,1,0:T(8,128)(2,1)S(1)} %get-tuple-element.5), channel_id=1, source_target_pairs={{0,8},{2,10},{4,12},{6,14},{8,16},{10,18},{12,20},{14,22},{16,24},... | collective-permute-start | bytes 196616 | tf_op jit(solution)/shard_map/ppermute | solution.py:130
Sparse Core Ops, SparseCore 0:
  18.7 22.9 all-gather.1
  64.9 47.2 reduce-scatter.1

commit v2 on v1

--- a/solution.py
+++ b/solution.py
@@ -78,22 +78,25 @@
             return carry
 
         lax.fori_loop(0, (count + BATCH - 1) // BATCH, one_batch, 0)
+        groups, depth = grad_ref.shape[0], grad_ref.shape[3]
         for tap in range(9):
-            part = slice(tap * channels, (tap + 1) * channels)
-            grad_ref[c, part, :] = acc[:, part].T.astype(grad_ref.dtype)
+            part = acc[:, tap * channels : (tap + 1) * channels].T.astype(grad_ref.dtype)
+            grad_ref[:, c, tap] = part.reshape(groups, depth, species)
         return carry
 
     lax.fori_loop(0, clusters, one_cluster, 0)
 
 
-def gradient_shares(group, lists, rows, weights, labels):
+def gradient_shares(groups, group, lists, rows, weights, labels):
     clusters, taps, channels, species = weights.shape
     rows_all, columns, _ = rows.shape
     smem = pl.BlockSpec(memory_space=pltpu.SMEM)
     vmem = pl.BlockSpec(memory_space=pltpu.VMEM)
     return pl.pallas_call(
         head_kernel,
-        out_shape=jax.ShapeDtypeStruct((clusters, taps * channels, species), jnp.bfloat16),
+        out_shape=jax.ShapeDtypeStruct(
+            (groups, clusters, taps, channels // groups, species), jnp.bfloat16
+        ),
         in_specs=[smem, smem, vmem, vmem, vmem],
         out_specs=vmem,
         scratch_shapes=[
@@ -113,38 +116,299 @@
     )
 
 
-def shards(members, features, weights, tile_lists, labels):
+def remote(src, dst, send, recv, space, clus):
+    return pltpu.make_async_remote_copy(
+        src_ref=src,
+        dst_ref=dst,
+        send_sem=send,
+        recv_sem=recv,
+        device_id=(space, clus),
+        device_id_type=pl.DeviceIdType.MESH,
+    )
+
+
+def greet(space, clus):
+    barrier = pltpu.get_barrier_semaphore()
+    pl.semaphore_signal(
+        barrier, inc=1, device_id=(space, clus), device_id_type=pl.DeviceIdType.MESH
+    )
+
+
+def gather_kernel(
+    members, groups, sides, own_ref, rows_ref, zeros, send, passed, recv, edge_send, edge_recv, local
+):
+    me, side = lax.axis_index("space"), lax.axis_index("clus")
+    group, member = me // members, me % members
+    pair, core = member // 2, member % 2
+    pairs = members // 2
+    first = group * members
+    sibling = first + pair * 2 + 1 - core
+    width = own_ref.shape[1]
+    last = rows_ref.shape[0] - 1
+    offsets = [(a, b) for a in range(pairs) for b in range(sides) if (a, b) != (0, 0)]
+
+    def spot(j, v):
+        return rows_ref.at[pl.ds(1 + j * SIDE, SIDE), pl.ds(pl.multiple_of(v * width, width), width)]
+
+    def edge(row, v):
+        return rows_ref.at[pl.ds(row, 1), pl.ds(pl.multiple_of(v * width, width), width)]
+
+    def towards(a, b):
+        return first + lax.rem(pair + a, pairs) * 2 + core, lax.rem(side + b, sides)
+
+    def origin(a, b):
+        return lax.rem(pair + pairs - a, pairs) * 2 + core, lax.rem(side + sides - b, sides)
+
+    for a, b in offsets:
+        j, v = origin(a, b)
+        greet(first + j, v)
+    greet(sibling, side)
+
+    @pl.when(group > 0)
+    def _():
+        for v in range(sides):
+            greet(first - 1, v)
+
+    @pl.when(group < groups - 1)
+    def _():
+        for v in range(sides):
+            greet(first + members, v)
+
+    sends_up = (member == members - 1) & (group < groups - 1)
+    sends_down = (member == 0) & (group > 0)
+    barrier = pltpu.get_barrier_semaphore()
+    edges = (sends_up | sends_down).astype(jnp.int32) * (members * sides)
+    pl.semaphore_wait(barrier, len(offsets) + 1 + edges)
+
+    here = recv.at[member * sides + side]
+    copies = []
+    for i, (a, b) in enumerate(offsets):
+        space, clus = towards(a, b)
+        copies.append(remote(own_ref, spot(member, side), send.at[i], here, space, clus))
+    copies.append(
+        remote(own_ref, spot(member, side), send.at[len(offsets)], here, sibling, side)
+    )
+    for copy in copies:
+        copy.start()
+    keep = pltpu.make_async_copy(own_ref, spot(member, side), local.at[0])
+    keep.start()
+
+    def edge_copies(up):
+        src = own_ref.at[pl.ds(SIDE - 1 if up else 0, 1)]
+        start = first + members if up else first - members
+        row, d = (0, 0) if up else (last, 1)
+        return [
+            remote(
+                src,
+                edge(row, side),
+                edge_send.at[d * members * sides + j * sides + v],
+                edge_recv.at[d * sides + side],
+                start + j,
+                v,
+            )
+            for j in range(members)
+            for v in range(sides)
+        ]
+
+    @pl.when(sends_up)
+    def _():
+        for copy in edge_copies(True):
+            copy.start()
+
+    @pl.when(sends_down)
+    def _():
+        for copy in edge_copies(False):
+            copy.start()
+
+    zeros[...] = jnp.zeros_like(zeros)
+
+    @pl.when(group == 0)
+    def _():
+        blank = pltpu.make_async_copy(zeros, rows_ref.at[pl.ds(0, 1)], local.at[1])
+        blank.start()
+        blank.wait()
+
+    @pl.when(group == groups - 1)
+    def _():
+        blank = pltpu.make_async_copy(zeros, rows_ref.at[pl.ds(last, 1)], local.at[2])
+        blank.start()
+        blank.wait()
+
+    for i, (a, b) in enumerate(offsets):
+        j, v = origin(a, b)
+        mark = recv.at[j * sides + v]
+        block = remote(spot(j, v), spot(j, v), passed.at[i], mark, sibling, side)
+        block.wait_recv()
+        block.start()
+        copies.append(block)
+    for a in range(pairs):
+        for b in range(sides):
+            j, v = a * 2 + 1 - core, b
+            mark = recv.at[j * sides + v]
+            remote(spot(j, v), spot(j, v), passed.at[0], mark, sibling, side).wait_recv()
+
+    @pl.when(group > 0)
+    def _():
+        for v in range(sides):
+            remote(edge(0, v), edge(0, v), edge_send.at[0], edge_recv.at[v], sibling, side).wait_recv()
+
+    @pl.when(group < groups - 1)
+    def _():
+        for v in range(sides):
+            mark = edge_recv.at[sides + v]
+            remote(edge(last, v), edge(last, v), edge_send.at[0], mark, sibling, side).wait_recv()
+
+    keep.wait()
+    for copy in copies:
+        copy.wait_send()
+
+    @pl.when(sends_up)
+    def _():
+        for copy in edge_copies(True):
+            copy.wait_send()
+
+    @pl.when(sends_down)
+    def _():
+        for copy in edge_copies(False):
+            copy.wait_send()
+
+
+def group_rows(members, groups, sides, features):
+    side_rows, width, channels = features.shape
+    count = members * sides
+    dma = pltpu.SemaphoreType.DMA
+    return pl.pallas_call(
+        functools.partial(gather_kernel, members, groups, sides),
+        out_shape=jax.ShapeDtypeStruct(
+            (members * side_rows + 2, sides * width, channels), features.dtype
+        ),
+        in_specs=[pl.BlockSpec(memory_space=pl.ANY)],
+        out_specs=pl.BlockSpec(memory_space=pl.ANY),
+        scratch_shapes=[
+            pltpu.VMEM((1, sides * width, channels), features.dtype),
+            dma((count,)),
+            dma((count,)),
+            dma((count,)),
+            dma((2 * count,)),
+            dma((2 * sides,)),
+            dma((3,)),
+        ],
+        compiler_params=pltpu.CompilerParams(collective_id=0, has_side_effects=True),
+        cost_estimate=pl.CostEstimate(flops=0, bytes_accessed=4 * 10**6, transcendentals=0),
+    )(features)
+
+
+def reduce_kernel(
+    members, groups, step, share_ref, old_ref, new_ref, landed, fresh, send, recv, out_send, out_recv, local
+):
+    me, side = lax.axis_index("space"), lax.axis_index("clus")
+    group, member = me // members, me % members
+    clusters, taps, depth, species = old_ref.shape
+    piece = depth // members
+    others = groups - 1
+
+    for o in range(1, groups):
+        greet(lax.rem(group + o, groups) * members + member, side)
+    for o in range(1, members):
+        greet(group * members + lax.rem(member + o, members), side)
+    pl.semaphore_wait(pltpu.get_barrier_semaphore(), groups - 1 + members - 1)
+
+    def part(c, o):
+        to = lax.rem(group + o, groups)
+        i = c * others + o - 1
+        return remote(
+            share_ref.at[to, c], landed.at[o - 1, c], send.at[i], recv.at[i], to * members + member, side
+        )
+
+    def handed(c, o):
+        to = lax.rem(member + o, members)
+        i = c * members + o
+        return remote(
+            fresh.at[to, c],
+            new_ref.at[member * clusters + c],
+            out_send.at[i],
+            out_recv.at[i],
+            group * members + to,
+            side,
+        )
+
+    def kept(c):
+        return pltpu.make_async_copy(
+            fresh.at[member, c], new_ref.at[member * clusters + c], local.at[c]
+        )
+
+    for c in range(clusters):
+        for o in range(1, groups):
+            part(c, o).start()
+    for c in range(clusters):
+        for o in range(1, groups):
+            part(c, o).wait_recv()
+
+        def one_tap(tap, carry, c=c):
+            total = share_ref[group, c, tap].astype(jnp.float32)
+            for o in range(1, groups):
+                total = total + landed[o - 1, c, tap].astype(jnp.float32)
+            new = old_ref[c, tap].astype(jnp.float32) - step * total
+            fresh[:, c, tap] = new.reshape(members, piece, species).astype(fresh.dtype)
+            return carry
+
+        lax.fori_loop(0, taps, one_tap, 0)
+        for o in range(1, members):
+            handed(c, o).start()
+        kept(c).start()
+    for c in range(clusters):
+        kept(c).wait()
+        for o in range(1, members):
+            handed(c, o).wait()
+        for o in range(1, groups):
+            part(c, o).wait_send()
+
+
+def new_shares(members, step, share, old):
+    groups, clusters, taps, depth, species = share.shape
+    vmem = pl.BlockSpec(memory_space=pltpu.VMEM)
+    dma = pltpu.SemaphoreType.DMA
+    return pl.pallas_call(
+        functools.partial(reduce_kernel, members, groups, step),
+        out_shape=jax.ShapeDtypeStruct(
+            (members * clusters, taps, depth // members, species), old.dtype
+        ),
+        in_specs=[vmem, vmem],
+        out_specs=vmem,
+        scratch_shapes=[
+            pltpu.VMEM((groups - 1, clusters, taps, depth, species), share.dtype),
+            pltpu.VMEM((members, clusters, taps, depth // members, species), old.dtype),
+            dma((clusters * (groups - 1),)),
+            dma((clusters * (groups - 1),)),
+            dma((clusters * members,)),
+            dma((clusters * members,)),
+            dma((clusters,)),
+        ],
+        compiler_params=pltpu.CompilerParams(
+            collective_id=1, has_side_effects=True, vmem_limit_bytes=24 * 2**20
+        ),
+        cost_estimate=pl.CostEstimate(flops=10**6, bytes_accessed=4 * 10**6, transcendentals=0),
+    )(share, old)
+
+
+def shards(members, sides, features, weights, tile_lists, labels):
     spaces = lax.axis_size("space")
     position = lax.axis_index("space")
     groups = spaces // members
     group, member = position // members, position % members
-    inner = [[g * members + j for j in range(members)] for g in range(groups)]
-    outer = [[g * members + j for g in range(groups)] for j in range(members)]
     clusters, taps, channels, species = weights.shape
     mine = clusters // members
 
-    rows = lax.all_gather(features, "clus", axis=1, tiled=True)
-    rows = lax.all_gather(rows, "space", axis=0, tiled=True, axis_index_groups=inner)
-    up = [(i, i + members) for i in range(spaces - members)]
-    down = [(j, i) for i, j in up]
-    before = lax.ppermute(rows[-1:], "space", up)
-    after = lax.ppermute(rows[:1], "space", down)
-    rows = jnp.concatenate([before, rows, after], axis=0)
-
+    rows = group_rows(members, groups, sides, features)
     own = lambda x: lax.dynamic_slice_in_dim(x, member * mine, mine, 0)
     own_weights = own(weights)
-    share = gradient_shares(group, own(tile_lists), rows, own_weights, own(labels))
-    share = share.reshape(mine, taps, channels, species)
-    total = lax.psum_scatter(
-        share, "space", scatter_dimension=2, axis_index_groups=outer, tiled=True
-    ).astype(jnp.float32)
+    share = gradient_shares(groups, group, own(tile_lists), rows, own_weights, own(labels))
     step = math.sqrt(9 * channels * SIDE * SIDE / tile_lists.shape[1]) / math.sqrt(9 * channels)
     depth = channels // groups
-    old = lax.dynamic_slice_in_dim(own_weights, group * depth, depth, 2).astype(jnp.float32)
-    new = (old - step * total).astype(jnp.bfloat16)
-    return lax.all_to_all(
-        new, "space", split_axis=2, concat_axis=0, axis_index_groups=inner, tiled=True
-    )
+    old = lax.dynamic_slice(
+        weights, (member * mine, 0, group * depth, 0), (mine, taps, depth, species)
+    )
+    return new_shares(members, step, share, old)
 
 
 def solution(mesh):
@@ -155,9 +419,9 @@
         P("clus", None, None),
     )
     out_specs = P("clus", None, "space", None)
-    members = math.gcd(4, mesh.shape["space"])
+    members = 4
     return jax.shard_map(
-        functools.partial(shards, members),
+        functools.partial(shards, members, mesh.shape["clus"]),
         mesh=mesh,
         in_specs=in_specs,
         out_specs=out_specs,

time: 133 us -> 69.3 us (0.52)
  the two profiles are of different devices: /device:TPU:0 before, /device:TPU:9 now
where the time goes in v2:
time: 69.3 us; the launch traced here: 69.4 us
  Pallas kernels  63.9 us (92%)
  local copies, waits for them, and re-layouts  5.44 us (8%)
    pallas_call x1, Pallas kernels, new_shares(): pl.pallas_call(functools.partial(reduce_kernel, members, groups, step), o...  33.1 us
    pallas_call x1, Pallas kernels, group_rows(): pl.pallas_call(functools.partial(gather_kernel, members, groups, sides),...  19.6 us
    pallas_call x1, Pallas kernels, gradient_shares(): pl.pallas_call(head_kernel, out_shape=jax.ShapeDtypeStruct((groups, clust...  11.2 us
    unnamed x5, local copies, waits for them, and re-layouts  2.34 us
    dynamic_slice x3, local copies, waits for them, and re-layouts, shards(): own = lambda x: lax.dynamic_slice_in_dim(x, member * mine, mine, 0)  2.1 us

profile of v2, /device:TPU:9, one launch (start us, length us, event | category | flops | bytes accessed | tf_op | source)
XLA Modules:
  0.0 69.4 jit_solution(3936197681200790521)
XLA Ops:
  0.0 0.0 copy-start
  0.0 1.4 %constant_dynamic-slice_fusion.2 = bf16[2,9,256,128]{3,2,1,0:T(8,128)(2,1)S(1)} fusion(bf16[8,9,256,128]{3,2,1,0:T(8,128)(2,1)} %param.5, s32[]{:T(128)S(6)} %select_n.22), kind=kLoop, calls=%fused_computation.2 | loop fusion | bytes 2359300 | tf_op jit(solution)/shard_map/dynamic_slice | solution.py:403
  1.4 0.0 copy-done
  1.4 0.7 %constant_dynamic-slice_fusion.3.lists_ref = s32[2,64]{1,0:T(2,128)S(1)} fusion(s32[8,64]{1,0:T(8,128)} %param.6, s32[]{:T(128)S(6)} %select_n.22), kind=kLoop, calls=%fused_computation.3 | loop fusion | bytes 1028 | tf_op jit(solution)/shard_map/dynamic_slice | solution.py:403
  2.1 19.6 %shard_map.46.map_ref = bf16[34,128,256]{2,1,0:T(8,128)(2,1)} custom-call(bf16[8,64,256]{2,1,0:T(8,128)(2,1)} %own_ref.1), custom_call_target="tpu_custom_call" | custom-call | bytes 4000000 | tf_op jit(solution)/shard_map/pallas_call | solution.py:280
  21.8 0.0 copy-start.1
  21.8 1.6 %copy-done.1 = bf16[34,128,256]{2,1,0:T(8,128)(2,1)S(1)} copy-done((bf16[34,128,256]{2,1,0:T(8,128)(2,1)S(1)}, bf16[34,128,256]{2,1,0:T(8,128)(2,1)}, u32[]{:S(2)}) %copy-start.1) | copy-done | bytes 2228248
  23.4 11.2 %shard_map.47.share_ref = bf16[4,2,9,64,128]{4,3,2,1,0:T(8,128)(2,1)S(1)} custom-call(s32[1]{0:T(128)} %bitcast.group_ref, s32[2,64]{1,0:T(2,128)S(1)} %constant_dynamic-slice_fusion.3.lists_ref, bf16[34,128,256]{2,1,0:T(8,128)(2,1)S(1)} %copy-done.1, bf16[2,2304,128]{2,1,0:T(8,128)(2,1)S(1)} %bitcast.3, s32[2,64,1,128]{3,2,1,0:T(1,128)S(1)} %bitcast.4), custom_call_target="tpu_custom_call" | custom-call | flops 5000000000 | bytes 6000000 | tf_op jit(solution)/shard_map/pallas_call | solution.py:95
  34.6 1.0 %constant_dynamic-slice_fusion.old_ref = bf16[2,9,64,128]{3,2,1,0:T(8,128)(2,1)S(1)} fusion(bf16[8,9,256,128]{3,2,1,0:T(8,128)(2,1)} %param.5, s32[]{:T(128)S(6)} %select_n.22, s32[]{:T(128)S(6)} %select_n.23), kind=kLoop, calls=%fused_computation | loop fusion | bytes 589832 | tf_op jit(solution)/shard_map/dynamic_slice | solution.py:408
  35.6 33.1 %shard_map.48 = bf16[8,9,16,128]{3,2,1,0:T(8,128)(2,1)S(1)} custom-call(bf16[4,2,9,64,128]{4,3,2,1,0:T(8,128)(2,1)S(1)} %shard_map.47.share_ref, bf16[2,9,64,128]{3,2,1,0:T(8,128)(2,1)S(1)} %constant_dynamic-slice_fusion.old_ref), custom_call_target="tpu_custom_call" | custom-call | flops 1000000 | bytes 4000000 | tf_op jit(solution)/shard_map/pallas_call | solution.py:371
  68.7 0.7 %copy.6 = bf16[8,9,16,128]{3,2,1,0:T(8,128)(2,1)} copy(bf16[8,9,16,128]{3,2,1,0:T(8,128)(2,1)S(1)} %shard_map.48) | data formatting | bytes 589824
  (1 shorter events, 0.0 us)
Async XLA Ops:
  0.0 1.4 %copy-start = (s32[8,64,128]{2,1,0:T(8,128)S(1)}, s32[8,64,128]{2,1,0:T(8,128)}, u32[]{:S(2)}) copy-start(s32[8,64,128]{2,1,0:T(8,128)} %param.7) | copy-start | bytes 786436
  21.8 1.6 %copy-start.1 = (bf16[34,128,256]{2,1,0:T(8,128)(2,1)S(1)}, bf16[34,128,256]{2,1,0:T(8,128)(2,1)}, u32[]{:S(2)}) copy-start(bf16[34,128,256]{2,1,0:T(8,128)(2,1)} %shard_map.46.map_ref) | copy-start | bytes 6684676

commit v3 on v2

--- a/solution.py
+++ b/solution.py
@@ -299,26 +299,91 @@
 
 
 def reduce_kernel(
-    members, groups, step, share_ref, old_ref, new_ref, landed, fresh, send, recv, out_send, out_recv, local
+    members,
+    groups,
+    step,
+    share_ref,
+    weights_ref,
+    new_ref,
+    old,
+    near,
+    relay,
+    joined,
+    far,
+    fresh,
+    near_send,
+    near_recv,
+    relay_send,
+    relay_recv,
+    far_send,
+    far_recv,
+    out_send,
+    out_recv,
+    local,
 ):
     me, side = lax.axis_index("space"), lax.axis_index("clus")
     group, member = me // members, me % members
-    clusters, taps, depth, species = old_ref.shape
+    clusters, taps, depth, species = old.shape
     piece = depth // members
-    others = groups - 1
-
-    for o in range(1, groups):
-        greet(lax.rem(group + o, groups) * members + member, side)
+    pairs = groups // 2
+    pair = group // 2
+
+    def joint_of(p):
+        return p * 2 + (p < pairs // 2).astype(jnp.int32)
+
+    def at(g):
+        return g * members + member
+
+    partner = pair * 2 + 1 - group % 2
+    is_joint = group == joint_of(pair)
+    not_joint = group != joint_of(pair)
+
+    kept_weights = pltpu.make_async_copy(
+        weights_ref.at[
+            pl.ds(member * clusters, clusters),
+            :,
+            pl.ds(pl.multiple_of(group * depth, depth), depth),
+        ],
+        old,
+        local.at[clusters],
+    )
+    kept_weights.start()
+
+    greet(at(partner), side)
+    for q in range(1, pairs):
+        greet(at(joint_of(lax.rem(pair + q, pairs))), side)
     for o in range(1, members):
         greet(group * members + lax.rem(member + o, members), side)
-    pl.semaphore_wait(pltpu.get_barrier_semaphore(), groups - 1 + members - 1)
-
-    def part(c, o):
-        to = lax.rem(group + o, groups)
-        i = c * others + o - 1
+    pl.semaphore_wait(
+        pltpu.get_barrier_semaphore(), members + is_joint.astype(jnp.int32) * (2 * (pairs - 1))
+    )
+
+    parts = [(c, q, e) for c in range(clusters) for q in range(1, pairs) for e in range(2)]
+
+    def index(c, q, e):
+        return (c * (pairs - 1) + q - 1) * 2 + e
+
+    def to_partner(c):
         return remote(
-            share_ref.at[to, c], landed.at[o - 1, c], send.at[i], recv.at[i], to * members + member, side
+            share_ref.at[partner, c], near.at[c], near_send.at[c], near_recv.at[c], at(partner), side
         )
+
+    def to_joint(c, q, e):
+        i = index(c, q, e)
+        return remote(
+            share_ref.at[lax.rem(pair + q, pairs) * 2 + e, c],
+            relay.at[i],
+            relay_send.at[i],
+            relay_recv.at[i],
+            at(partner),
+            side,
+        )
+
+    def across(c, q, e):
+        i = index(c, q, e)
+        j = c * (pairs - 1) + q - 1
+        to = lax.rem(pair + q, pairs) * 2 + e
+        return remote(joined.at[i], far.at[j], far_send.at[i], far_recv.at[j], at(to), side)
 
     def handed(c, o):
         to = lax.rem(member + o, members)
@@ -337,18 +402,39 @@
             fresh.at[member, c], new_ref.at[member * clusters + c], local.at[c]
         )
 
+    @pl.when(not_joint)
+    def _():
+        for c, q, e in parts:
+            to_joint(c, q, e).start()
+
     for c in range(clusters):
-        for o in range(1, groups):
-            part(c, o).start()
+        to_partner(c).start()
+
+    @pl.when(is_joint)
+    def _():
+        for c, q, e in parts:
+            to_joint(c, q, e).wait_recv()
+            i, to = index(c, q, e), lax.rem(pair + q, pairs) * 2 + e
+
+            def join(tap, carry, i=i, to=to, c=c):
+                total = share_ref[to, c, tap].astype(jnp.float32) + relay[i, tap].astype(jnp.float32)
+                joined[i, tap] = total.astype(joined.dtype)
+                return carry
+
+            lax.fori_loop(0, taps, join, 0)
+            across(c, q, e).start()
+
+    kept_weights.wait()
     for c in range(clusters):
-        for o in range(1, groups):
-            part(c, o).wait_recv()
+        to_partner(c).wait_recv()
+        for q in range(1, pairs):
+            across(c, q, 0).wait_recv()
 
         def one_tap(tap, carry, c=c):
-            total = share_ref[group, c, tap].astype(jnp.float32)
-            for o in range(1, groups):
-                total = total + landed[o - 1, c, tap].astype(jnp.float32)
-            new = old_ref[c, tap].astype(jnp.float32) - step * total
+            total = share_ref[group, c, tap].astype(jnp.float32) + near[c, tap].astype(jnp.float32)
+            for q in range(1, pairs):
+                total = total + far[c * (pairs - 1) + q - 1, tap].astype(jnp.float32)
+            new = old[c, tap].astype(jnp.float32) - step * total
             fresh[:, c, tap] = new.reshape(members, piece, species).astype(fresh.dtype)
             return carry
 
@@ -360,35 +446,54 @@
         kept(c).wait()
         for o in range(1, members):
             handed(c, o).wait()
-        for o in range(1, groups):
-            part(c, o).wait_send()
-
-
-def new_shares(members, step, share, old):
+        to_partner(c).wait_send()
+
+    @pl.when(not_joint)
+    def _():
+        for c, q, e in parts:
+            to_joint(c, q, e).wait_send()
+
+    @pl.when(is_joint)
+    def _():
+        for c, q, e in parts:
+            across(c, q, e).wait_send()
+
+
+def new_shares(members, step, share, weights):
     groups, clusters, taps, depth, species = share.shape
+    away = clusters * (groups // 2 - 1)
+    block = (taps, depth, species)
+    dma = pltpu.SemaphoreType.DMA
     vmem = pl.BlockSpec(memory_space=pltpu.VMEM)
-    dma = pltpu.SemaphoreType.DMA
     return pl.pallas_call(
         functools.partial(reduce_kernel, members, groups, step),
         out_shape=jax.ShapeDtypeStruct(
-            (members * clusters, taps, depth // members, species), old.dtype
+            (members * clusters, taps, depth // members, species), weights.dtype
         ),
-        in_specs=[vmem, vmem],
+        in_specs=[vmem, pl.BlockSpec(memory_space=pl.ANY)],
         out_specs=vmem,
         scratch_shapes=[
-            pltpu.VMEM((groups - 1, clusters, taps, depth, species), share.dtype),
-            pltpu.VMEM((members, clusters, taps, depth // members, species), old.dtype),
-            dma((clusters * (groups - 1),)),
-            dma((clusters * (groups - 1),)),
+            pltpu.VMEM((clusters,) + block, weights.dtype),
+            pltpu.VMEM((clusters,) + block, share.dtype),
+            pltpu.VMEM((2 * away,) + block, share.dtype),
+            pltpu.VMEM((2 * away,) + block, share.dtype),
+            pltpu.VMEM((away,) + block, share.dtype),
+            pltpu.VMEM((members, clusters, taps, depth // members, species), weights.dtype),
+            dma((clusters,)),
+            dma((clusters,)),
+            dma((2 * away,)),
+            dma((2 * away,)),
+            dma((2 * away,)),
+            dma((away,)),
             dma((clusters * members,)),
             dma((clusters * members,)),
-            dma((clusters,)),
+            dma((clusters + 1,)),
         ],
         compiler_params=pltpu.CompilerParams(
             collective_id=1, has_side_effects=True, vmem_limit_bytes=24 * 2**20
         ),
         cost_estimate=pl.CostEstimate(flops=10**6, bytes_accessed=4 * 10**6, transcendentals=0),
-    )(share, old)
+    )(share, weights)
 
 
 def shards(members, sides, features, weights, tile_lists, labels):
@@ -404,11 +509,7 @@
     own_weights = own(weights)
     share = gradient_shares(groups, group, own(tile_lists), rows, own_weights, own(labels))
     step = math.sqrt(9 * channels * SIDE * SIDE / tile_lists.shape[1]) / math.sqrt(9 * channels)
-    depth = channels // groups
-    old = lax.dynamic_slice(
-        weights, (member * mine, 0, group * depth, 0), (mine, taps, depth, species)
-    )
-    return new_shares(members, step, share, old)
+    return new_shares(members, step, share, weights)
 
 
 def solution(mesh):

time: 69.3 us -> 63.1 us (0.911)
  the two profiles are of different devices: /device:TPU:9 before, /device:TPU:17 now
where the time goes in v3:
time: 63.1 us; the launch traced here: 63.8 us
  Pallas kernels  59.1 us (94%)
  local copies, waits for them, and re-layouts  4.67 us (7%)
    pallas_call x1, Pallas kernels, new_shares(): pl.pallas_call(functools.partial(reduce_kernel, members, groups, step), o...  28.2 us
    pallas_call x1, Pallas kernels, group_rows(): pl.pallas_call(functools.partial(gather_kernel, members, groups, sides),...  19.6 us
    pallas_call x1, Pallas kernels, gradient_shares(): pl.pallas_call(head_kernel, out_shape=jax.ShapeDtypeStruct((groups, clust...  11.2 us
    unnamed x9, local copies, waits for them, and re-layouts  2.58 us
    dynamic_slice x3, local copies, waits for them, and re-layouts, shards(): own = lambda x: lax.dynamic_slice_in_dim(x, member * mine, mine, 0)  2.09 us

profile of v3, /device:TPU:17, one launch (start us, length us, event | category | flops | bytes accessed | tf_op | source)
XLA Modules:
  0.0 63.8 jit_solution(11241732702106271127)
XLA Ops:
  0.0 0.0 copy-start
  0.0 0.7 %constant_dynamic-slice_fusion.2.lists_ref = s32[2,64]{1,0:T(2,128)S(1)} fusion(s32[8,64]{1,0:T(8,128)} %param.6, s32[]{:T(128)S(6)} %select_n.18), kind=kLoop, calls=%fused_computation.2 | loop fusion | bytes 1028 | tf_op jit(solution)/shard_map/dynamic_slice | solution.py:508
  0.7 0.2 copy-done
  1.0 1.3 %constant_dynamic-slice_fusion.1 = bf16[2,9,256,128]{3,2,1,0:T(8,128)(2,1)S(1)} fusion(bf16[8,9,256,128]{3,2,1,0:T(8,128)(2,1)} %weights_ref.1, s32[]{:T(128)S(6)} %select_n.18), kind=kLoop, calls=%fused_computation.1 | loop fusion | bytes 2359300 | tf_op jit(solution)/shard_map/dynamic_slice | solution.py:508
  2.3 0.0 slice-start
  2.3 19.6 %shard_map.46.map_ref = bf16[34,128,256]{2,1,0:T(8,128)(2,1)} custom-call(bf16[8,64,256]{2,1,0:T(8,128)(2,1)} %own_ref.1), custom_call_target="tpu_custom_call" | custom-call | bytes 4000000 | tf_op jit(solution)/shard_map/pallas_call | solution.py:280
  22.0 0.0 copy-start.1
  22.0 1.6 %copy-done.1 = bf16[34,128,256]{2,1,0:T(8,128)(2,1)S(1)} copy-done((bf16[34,128,256]{2,1,0:T(8,128)(2,1)S(1)}, bf16[34,128,256]{2,1,0:T(8,128)(2,1)}, u32[]{:S(2)}) %copy-start.1) | copy-done | bytes 2228248
  23.6 0.0 slice-start.1
  23.6 11.2 %shard_map.47.share_ref = bf16[4,2,9,64,128]{4,3,2,1,0:T(8,128)(2,1)S(1)} custom-call(s32[1]{0:T(128)} %bitcast.group_ref, s32[2,64]{1,0:T(2,128)S(1)} %constant_dynamic-slice_fusion.2.lists_ref, bf16[34,128,256]{2,1,0:T(8,128)(2,1)S(1)} %copy-done.1, bf16[2,2304,128]{2,1,0:T(8,128)(2,1)S(1)} %bitcast.5, s32[2,64,1,128]{3,2,1,0:T(1,128)S(1)} %bitcast.6), custom_call_target="tpu_custom_call" | custom-call | flops 5000000000 | bytes 6000000 | tf_op jit(solution)/shard_map/pallas_call | solution.py:95
  34.9 0.0 slice-done
  34.9 0.0 slice-done.1
  34.9 28.2 %shard_map.48 = bf16[8,9,16,128]{3,2,1,0:T(8,128)(2,1)S(1)} custom-call(bf16[4,2,9,64,128]{4,3,2,1,0:T(8,128)(2,1)S(1)} %shard_map.47.share_ref, bf16[8,9,256,128]{3,2,1,0:T(8,128)(2,1)S(1)} %bitcast.4), custom_call_target="tpu_custom_call" | custom-call | flops 1000000 | bytes 4000000 | tf_op jit(solution)/shard_map/pallas_call | solution.py:468
  63.1 0.7 %copy.6 = bf16[8,9,16,128]{3,2,1,0:T(8,128)(2,1)} copy(bf16[8,9,16,128]{3,2,1,0:T(8,128)(2,1)S(1)} %shard_map.48) | data formatting | bytes 589824
  (2 shorter events, 0.0 us)
Async XLA Ops:
  0.0 1.0 %copy-start = (s32[8,64,128]{2,1,0:T(8,128)S(1)}, s32[8,64,128]{2,1,0:T(8,128)}, u32[]{:S(2)}) copy-start(s32[8,64,128]{2,1,0:T(8,128)} %param.7) | copy-start | bytes 786436
  2.3 32.6 %slice-start = ((s8[4718592]{0:T(1024)(128)(4,1)}), s8[524288]{0:T(1024)(128)(4,1)S(1)}, s32[]{:S(2)}) async-start(s8[4718592]{0:T(1024)(128)(4,1)} %bitcast.3), calls=%async_computation | async-start | bytes 1048576
  22.0 1.6 %copy-start.1 = (bf16[34,128,256]{2,1,0:T(8,128)(2,1)S(1)}, bf16[34,128,256]{2,1,0:T(8,128)(2,1)}, u32[]{:S(2)}) copy-start(bf16[34,128,256]{2,1,0:T(8,128)(2,1)} %shard_map.46.map_ref) | copy-start | bytes 6684676
  23.6 11.3 %slice-start.1 = ((s8[4718592]{0:T(1024)(128)(4,1)}), s8[4194304]{0:T(1024)(128)(4,1)S(1)}, s32[]{:S(2)}) async-start(s8[4718592]{0:T(1024)(128)(4,1)} %bitcast.3), calls=%async_computation.1 | async-start | bytes 8388608

commit v4 on v3

--- a/solution.py
+++ b/solution.py
@@ -12,14 +12,24 @@
 BATCH = 4
 
 
-def head_kernel(group_ref, lists_ref, map_ref, weights_ref, labels_ref, grad_ref, wide, cols, acc, chosen):
-    clusters, length = lists_ref.shape
+def head_kernel(
+    members, lists_ref, map_ref, weights_all, labels_all, grad_ref, wide, cols, acc, chosen, weights_ref, labels_ref, sems
+):
+    me = lax.axis_index("space")
+    group, member = me // members, me % members
+    clusters, length = labels_ref.shape[0], labels_ref.shape[1]
+    mine = pl.ds(member * clusters, clusters)
+    fetches = [
+        pltpu.make_async_copy(weights_all.at[mine], weights_ref, sems.at[0]),
+        pltpu.make_async_copy(labels_all.at[mine], labels_ref, sems.at[1]),
+    ]
+    for fetch in fetches:
+        fetch.start()
     rows_all, columns, channels = map_ref.shape
     tiles = columns // SIDE
     bands = (rows_all - 2) // SIDE
     per_group = tiles * bands
     species = weights_ref.shape[2]
-    group = group_ref[0]
     scaling = 1.0 / math.sqrt(9 * channels)
     cells = SIDE * SIDE
 
@@ -30,12 +40,14 @@
         return carry
 
     lax.fori_loop(0, rows_all, widen, 0)
+    for fetch in fetches:
+        fetch.wait()
     side_row = lax.broadcasted_iota(jnp.int32, (SIDE + 2, SIDE, channels), 1)
 
     def one_cluster(c, carry):
         def choose(k, count):
             chosen[count] = k
-            return count + (lists_ref[c, k] // per_group == group).astype(jnp.int32)
+            return count + (lists_ref[member * clusters + c, k] // per_group == group).astype(jnp.int32)
 
         count = lax.fori_loop(0, length, choose, jnp.int32(0))
         acc[...] = jnp.zeros_like(acc)
@@ -45,7 +57,7 @@
             for j in range(BATCH):
                 slot = b * BATCH + j
                 k = chosen[jnp.minimum(slot, count - 1)]
-                tile = lists_ref[c, k] - group * per_group
+                tile = lists_ref[member * clusters + c, k] - group * per_group
                 band, column = tile // tiles, tile % tiles
                 rows = pl.ds(band * SIDE, SIDE + 2)
                 left, mid, right = wide[rows, column], wide[rows, column + 1], wide[rows, column + 2]
@@ -65,7 +77,7 @@
                         cols[j * cells : (j + 1) * cells, tap * channels : (tap + 1) * channels] = flat[
                             dy * SIDE : dy * SIDE + cells
                         ].astype(jnp.bfloat16)
-                targets.append(jnp.broadcast_to(labels_ref[c, k].astype(jnp.float32), (cells, species)))
+                targets.append(jnp.broadcast_to(labels_ref[c, pl.ds(k, 1), :].astype(jnp.float32), (cells, species)))
             target = jnp.concatenate(targets, axis=0)
             logits = jnp.dot(cols[...], weights_ref[c], preferred_element_type=jnp.float32)
             probability = jax.nn.sigmoid(logits * scaling)
@@ -87,33 +99,32 @@
     lax.fori_loop(0, clusters, one_cluster, 0)
 
 
-def gradient_shares(groups, group, lists, rows, weights, labels):
-    clusters, taps, channels, species = weights.shape
+def gradient_shares(members, groups, lists, rows, weights, labels):
+    count, taps, channels, species = weights.shape
     rows_all, columns, _ = rows.shape
+    clusters = count // members
     smem = pl.BlockSpec(memory_space=pltpu.SMEM)
     vmem = pl.BlockSpec(memory_space=pltpu.VMEM)
+    whole = pl.BlockSpec(memory_space=pl.ANY)
     return pl.pallas_call(
-        head_kernel,
+        functools.partial(head_kernel, members),
         out_shape=jax.ShapeDtypeStruct(
             (groups, clusters, taps, channels // groups, species), jnp.bfloat16
         ),
-        in_specs=[smem, smem, vmem, vmem, vmem],
+        in_specs=[smem, vmem, whole, whole],
         out_specs=vmem,
         scratch_shapes=[
             pltpu.VMEM((rows_all, columns // SIDE + 2, SIDE, channels), jnp.float32),
             pltpu.VMEM((BATCH * SIDE * SIDE, taps * channels), jnp.bfloat16),
             pltpu.VMEM((species, taps * channels), jnp.float32),
             pltpu.SMEM((lists.shape[1],), jnp.int32),
+            pltpu.VMEM((clusters, taps * channels, species), weights.dtype),
+            pltpu.VMEM((clusters,) + labels.shape[1:], labels.dtype),
+            pltpu.SemaphoreType.DMA((2,)),
         ],
         compiler_params=pltpu.CompilerParams(vmem_limit_bytes=40 * 2**20),
         cost_estimate=pl.CostEstimate(flops=5 * 10**9, bytes_accessed=6 * 10**6, transcendentals=0),
-    )(
-        group.reshape(1),
-        lists,
-        rows,
-        weights.reshape(clusters, taps * channels, species),
-        labels.reshape(clusters, labels.shape[1], 1, species),
-    )
+    )(lists, rows, weights.reshape(count, taps * channels, species), labels)
 
 
 def remote(src, dst, send, recv, space, clus):
@@ -135,7 +146,7 @@
 
 
 def gather_kernel(
-    members, groups, sides, own_ref, rows_ref, zeros, send, passed, recv, edge_send, edge_recv, local
+    members, groups, sides, own_ref, rows_ref, send, passed, recv, edge_send, edge_recv, local
 ):
     me, side = lax.axis_index("space"), lax.axis_index("clus")
     group, member = me // members, me % members
@@ -188,11 +199,6 @@
     copies.append(
         remote(own_ref, spot(member, side), send.at[len(offsets)], here, sibling, side)
     )
-    for copy in copies:
-        copy.start()
-    keep = pltpu.make_async_copy(own_ref, spot(member, side), local.at[0])
-    keep.start()
-
     def edge_copies(up):
         src = own_ref.at[pl.ds(SIDE - 1 if up else 0, 1)]
         start = first + members if up else first - members
@@ -220,19 +226,18 @@
         for copy in edge_copies(False):
             copy.start()
 
-    zeros[...] = jnp.zeros_like(zeros)
+    for copy in copies:
+        copy.start()
+    keep = pltpu.make_async_copy(own_ref, spot(member, side), local.at[0])
+    keep.start()
 
     @pl.when(group == 0)
     def _():
-        blank = pltpu.make_async_copy(zeros, rows_ref.at[pl.ds(0, 1)], local.at[1])
-        blank.start()
-        blank.wait()
+        rows_ref[0] = jnp.zeros_like(rows_ref[0])
 
     @pl.when(group == groups - 1)
     def _():
-        blank = pltpu.make_async_copy(zeros, rows_ref.at[pl.ds(last, 1)], local.at[2])
-        blank.start()
-        blank.wait()
+        rows_ref[last] = jnp.zeros_like(rows_ref[last])
 
     for i, (a, b) in enumerate(offsets):
         j, v = origin(a, b)
@@ -283,17 +288,18 @@
             (members * side_rows + 2, sides * width, channels), features.dtype
         ),
         in_specs=[pl.BlockSpec(memory_space=pl.ANY)],
-        out_specs=pl.BlockSpec(memory_space=pl.ANY),
+        out_specs=pl.BlockSpec(memory_space=pltpu.VMEM),
         scratch_shapes=[
-            pltpu.VMEM((1, sides * width, channels), features.dtype),
             dma((count,)),
             dma((count,)),
             dma((count,)),
             dma((2 * count,)),
             dma((2 * sides,)),
-            dma((3,)),
+            dma((1,)),
         ],
-        compiler_params=pltpu.CompilerParams(collective_id=0, has_side_effects=True),
+        compiler_params=pltpu.CompilerParams(
+            collective_id=0, has_side_effects=True, vmem_limit_bytes=16 * 2**20
+        ),
         cost_estimate=pl.CostEstimate(flops=0, bytes_accessed=4 * 10**6, transcendentals=0),
     )(features)
 
@@ -497,17 +503,10 @@
 
 
 def shards(members, sides, features, weights, tile_lists, labels):
-    spaces = lax.axis_size("space")
-    position = lax.axis_index("space")
-    groups = spaces // members
-    group, member = position // members, position % members
-    clusters, taps, channels, species = weights.shape
-    mine = clusters // members
-
+    groups = lax.axis_size("space") // members
+    channels = weights.shape[2]
     rows = group_rows(members, groups, sides, features)
-    own = lambda x: lax.dynamic_slice_in_dim(x, member * mine, mine, 0)
-    own_weights = own(weights)
-    share = gradient_shares(groups, group, own(tile_lists), rows, own_weights, own(labels))
+    share = gradient_shares(members, groups, tile_lists, rows, weights, labels)
     step = math.sqrt(9 * channels * SIDE * SIDE / tile_lists.shape[1]) / math.sqrt(9 * channels)
     return new_shares(members, step, share, weights)
 

time: 63.1 us -> 62.8 us (level); the launches traced: 63.8 us -> 62 us
  Pallas kernels: 59.1 us -> 58 us
  local copies, waits for them, and re-layouts: 4.67 us -> 4.01 us
    dynamic_slice x3 -> x0, local copies, waits for them, and re-layouts: 2.09 us -> none  [shards(): own = lambda x: lax.dynamic_slice_in_dim(x, member * mine, mine, 0)]
    unnamed x9, local copies, waits for them, and re-layouts: 2.58 us -> 4.01 us
    pallas_call x1, Pallas kernels: 28.2 us -> 27.3 us  [new_shares(): pl.pallas_call(functools.partial(reduce_kernel, members, groups, step), o...]
    pallas_call x1, Pallas kernels: 19.6 us -> 18.9 us  [group_rows(): pl.pallas_call(functools.partial(gather_kernel, members, groups, sides),...]
where the time goes in v4:
time: 62.8 us; the launch traced here: 62 us
  Pallas kernels  58 us (92%)
  local copies, waits for them, and re-layouts  4.01 us (6%)
    pallas_call x1, Pallas kernels, new_shares(): pl.pallas_call(functools.partial(reduce_kernel, members, groups, step), o...  27.3 us
    pallas_call x1, Pallas kernels, group_rows(): pl.pallas_call(functools.partial(gather_kernel, members, groups, sides),...  18.9 us
    pallas_call x1, Pallas kernels, gradient_shares(): pl.pallas_call(functools.partial(head_kernel, members), out_shape=jax.Sha...  11.8 us
    unnamed x9, local copies, waits for them, and re-layouts  4.01 us

profile of v4, /device:TPU:17, one launch (start us, length us, event | category | flops | bytes accessed | tf_op | source)
XLA Modules:
  0.0 62.0 jit_solution(6240357930343617478)
XLA Ops:
  0.0 0.0 copy-start.1
  0.0 0.9 %copy-done.1 = bf16[8,64,256]{2,1,0:T(8,128)(2,1)S(1)} copy-done((bf16[8,64,256]{2,1,0:T(8,128)(2,1)S(1)}, bf16[8,64,256]{2,1,0:T(8,128)(2,1)}, u32[]{:S(2)}) %copy-start.1) | copy-done | bytes 262168
  1.0 0.0 copy-start.2
  1.0 0.0 copy-start.3
  1.0 18.9 %shard_map.46.map_ref = bf16[34,128,256]{2,1,0:T(8,128)(2,1)S(1)} custom-call(bf16[8,64,256]{2,1,0:T(8,128)(2,1)S(1)} %copy-done.1), custom_call_target="tpu_custom_call" | custom-call | bytes 4000000 | tf_op jit(solution)/shard_map/pallas_call | solution.py:285
  19.9 0.0 copy-done.2
  19.9 0.0 copy-done.3
  19.9 0.0 copy-start
  19.9 2.3 %copy-done = bf16[8,9,256,128]{3,2,1,0:T(8,128)(2,1)S(1)} copy-done((bf16[8,9,256,128]{3,2,1,0:T(8,128)(2,1)S(1)}, bf16[8,9,256,128]{3,2,1,0:T(8,128)(2,1)}, u32[]{:S(2)}) %copy-start) | copy-done | bytes 4718616
  22.3 11.8 %shard_map.47.share_ref = bf16[4,2,9,64,128]{4,3,2,1,0:T(8,128)(2,1)S(1)} custom-call(s32[8,64]{1,0:T(8,128)S(1)} %copy-done.3, bf16[34,128,256]{2,1,0:T(8,128)(2,1)S(1)} %shard_map.46.map_ref, bf16[8,2304,128]{2,1,0:T(8,128)(2,1)S(1)} %bitcast.1, s32[8,64,128]{2,1,0:T(8,128)S(1)} %copy-done.2), custom_call_target="tpu_custom_call" | custom-call | flops 5000000000 | bytes 6000000 | tf_op jit(solution)/shard_map/pallas_call | solution.py:109
  34.0 27.3 %shard_map.48 = bf16[8,9,16,128]{3,2,1,0:T(8,128)(2,1)S(1)} custom-call(bf16[4,2,9,64,128]{4,3,2,1,0:T(8,128)(2,1)S(1)} %shard_map.47.share_ref, bf16[8,9,256,128]{3,2,1,0:T(8,128)(2,1)S(1)} %copy-done), custom_call_target="tpu_custom_call" | custom-call | flops 1000000 | bytes 4000000 | tf_op jit(solution)/shard_map/pallas_call | solution.py:474
  61.3 0.7 %copy.6 = bf16[8,9,16,128]{3,2,1,0:T(8,128)(2,1)} copy(bf16[8,9,16,128]{3,2,1,0:T(8,128)(2,1)S(1)} %shard_map.48) | data formatting | bytes 589824
Async XLA Ops:
  0.0 0.9 %copy-start.1 = (bf16[8,64,256]{2,1,0:T(8,128)(2,1)S(1)}, bf16[8,64,256]{2,1,0:T(8,128)(2,1)}, u32[]{:S(2)}) copy-start(bf16[8,64,256]{2,1,0:T(8,128)(2,1)} %own_ref.1) | copy-start | bytes 786436
  1.0 19.0 %copy-start.2 = (s32[8,64,128]{2,1,0:T(8,128)S(1)}, s32[8,64,128]{2,1,0:T(8,128)}, u32[]{:S(2)}) copy-start(s32[8,64,128]{2,1,0:T(8,128)} %labels_all.1) | copy-start | bytes 786436
  1.0 19.0 %copy-start.3 = (s32[8,64]{1,0:T(8,128)S(1)}, s32[8,64]{1,0:T(8,128)}, u32[]{:S(2)}) copy-start(s32[8,64]{1,0:T(8,128)} %lists_ref.1) | copy-start | bytes 6148
  19.9 2.3 %copy-start = (bf16[8,9,256,128]{3,2,1,0:T(8,128)(2,1)S(1)}, bf16[8,9,256,128]{3,2,1,0:T(8,128)(2,1)}, u32[]{:S(2)}) copy-start(bf16[8,9,256,128]{3,2,1,0:T(8,128)(2,1)} %weights_ref.1) | copy-start | bytes 14155780

commit v5 on v4

--- a/solution.py
+++ b/solution.py
@@ -105,7 +105,7 @@
     clusters = count // members
     smem = pl.BlockSpec(memory_space=pltpu.SMEM)
     vmem = pl.BlockSpec(memory_space=pltpu.VMEM)
-    whole = pl.BlockSpec(memory_space=pl.ANY)
+    whole = pl.BlockSpec(memory_space=pltpu.HBM)
     return pl.pallas_call(
         functools.partial(head_kernel, members),
         out_shape=jax.ShapeDtypeStruct(
@@ -146,33 +146,32 @@
 
 
 def gather_kernel(
-    members, groups, sides, own_ref, rows_ref, send, passed, recv, edge_send, edge_recv, local
+    members, groups, sides, own_ref, rows_ref, send, recv, edge_send, edge_recv, local
 ):
     me, side = lax.axis_index("space"), lax.axis_index("clus")
     group, member = me // members, me % members
     pair, core = member // 2, member % 2
-    pairs = members // 2
     first = group * members
     sibling = first + pair * 2 + 1 - core
     width = own_ref.shape[1]
     last = rows_ref.shape[0] - 1
-    offsets = [(a, b) for a in range(pairs) for b in range(sides) if (a, b) != (0, 0)]
-
-    def spot(j, v):
-        return rows_ref.at[pl.ds(1 + j * SIDE, SIDE), pl.ds(pl.multiple_of(v * width, width), width)]
+    half = SIDE // 2
+    opposite = (1 - pair) * 2 + core
+    across = [lax.rem(side + b, sides) for b in range(1, sides)]
+
+    def spot(j, v, h):
+        start = pl.multiple_of(v * width, width)
+        return rows_ref.at[pl.ds(1 + j * SIDE + h * half, half), pl.ds(start, width)]
+
+    def mark(j, v, h):
+        return recv.at[(j * sides + v) * 2 + h]
 
     def edge(row, v):
         return rows_ref.at[pl.ds(row, 1), pl.ds(pl.multiple_of(v * width, width), width)]
 
-    def towards(a, b):
-        return first + lax.rem(pair + a, pairs) * 2 + core, lax.rem(side + b, sides)
-
-    def origin(a, b):
-        return lax.rem(pair + pairs - a, pairs) * 2 + core, lax.rem(side + sides - b, sides)
-
-    for a, b in offsets:
-        j, v = origin(a, b)
-        greet(first + j, v)
+    for v in across:
+        greet(me, v)
+    greet(first + opposite, side)
     greet(sibling, side)
 
     @pl.when(group > 0)
@@ -189,16 +188,8 @@
     sends_down = (member == 0) & (group > 0)
     barrier = pltpu.get_barrier_semaphore()
     edges = (sends_up | sends_down).astype(jnp.int32) * (members * sides)
-    pl.semaphore_wait(barrier, len(offsets) + 1 + edges)
-
-    here = recv.at[member * sides + side]
-    copies = []
-    for i, (a, b) in enumerate(offsets):
-        space, clus = towards(a, b)
-        copies.append(remote(own_ref, spot(member, side), send.at[i], here, space, clus))
-    copies.append(
-        remote(own_ref, spot(member, side), send.at[len(offsets)], here, sibling, side)
-    )
+    pl.semaphore_wait(barrier, sides + 1 + edges)
+
     def edge_copies(up):
         src = own_ref.at[pl.ds(SIDE - 1 if up else 0, 1)]
         start = first + members if up else first - members
@@ -226,10 +217,32 @@
         for copy in edge_copies(False):
             copy.start()
 
-    for copy in copies:
+    sent = []
+
+    def hand(src, j, v, h, space, clus):
+        copy = remote(src, spot(j, v, h), send.at[len(sent)], mark(j, v, h), space, clus)
         copy.start()
-    keep = pltpu.make_async_copy(own_ref, spot(member, side), local.at[0])
-    keep.start()
+        sent.append(copy)
+
+    def arrived(j, v, h):
+        here = spot(j, v, h)
+        remote(here, here, send.at[0], mark(j, v, h), sibling, side).wait_recv()
+        return here
+
+    for h in range(2):
+        own = own_ref.at[pl.ds(h * half, half)]
+        other = own_ref.at[pl.ds((1 - h) * half, half)]
+        for v in across:
+            hand(own, member, side, h, me, v)
+        hand(other, member, side, 1 - h, first + opposite, side)
+    for h in range(2):
+        hand(own_ref.at[pl.ds(h * half, half)], member, side, h, sibling, side)
+    keep = [
+        pltpu.make_async_copy(own_ref.at[pl.ds(h * half, half)], spot(member, side, h), local.at[h])
+        for h in range(2)
+    ]
+    for copy in keep:
+        copy.start()
 
     @pl.when(group == 0)
     def _():
@@ -239,18 +252,24 @@
     def _():
         rows_ref[last] = jnp.zeros_like(rows_ref[last])
 
-    for i, (a, b) in enumerate(offsets):
-        j, v = origin(a, b)
-        mark = recv.at[j * sides + v]
-        block = remote(spot(j, v), spot(j, v), passed.at[i], mark, sibling, side)
-        block.wait_recv()
-        block.start()
-        copies.append(block)
-    for a in range(pairs):
-        for b in range(sides):
-            j, v = a * 2 + 1 - core, b
-            mark = recv.at[j * sides + v]
-            remote(spot(j, v), spot(j, v), passed.at[0], mark, sibling, side).wait_recv()
+    for v in across:
+        here = arrived(member, v, 0)
+        hand(here, member, v, 0, first + opposite, side)
+        hand(here, member, v, 0, sibling, side)
+    here = arrived(opposite, side, 1)
+    for v in across:
+        hand(here, opposite, side, 1, me, v)
+    hand(here, opposite, side, 1, sibling, side)
+    for v in across:
+        hand(arrived(member, v, 1), member, v, 1, sibling, side)
+    hand(arrived(opposite, side, 0), opposite, side, 0, sibling, side)
+    for v in across:
+        for h in range(2):
+            hand(arrived(opposite, v, h), opposite, v, h, sibling, side)
+    for p in range(2):
+        for v in range(sides):
+            for h in range(2):
+                arrived(p * 2 + 1 - core, v, h)
 
     @pl.when(group > 0)
     def _():
@@ -263,8 +282,9 @@
             mark = edge_recv.at[sides + v]
             remote(edge(last, v), edge(last, v), edge_send.at[0], mark, sibling, side).wait_recv()
 
-    keep.wait()
-    for copy in copies:
+    for copy in keep:
+        copy.wait()
+    for copy in sent:
         copy.wait_send()
 
     @pl.when(sends_up)
@@ -287,15 +307,14 @@
         out_shape=jax.ShapeDtypeStruct(
             (members * side_rows + 2, sides * width, channels), features.dtype
         ),
-        in_specs=[pl.BlockSpec(memory_space=pl.ANY)],
+        in_specs=[pl.BlockSpec(memory_space=pltpu.HBM)],
         out_specs=pl.BlockSpec(memory_space=pltpu.VMEM),
         scratch_shapes=[
-            dma((count,)),
-            dma((count,)),
-            dma((count,)),
+            dma((4 * count,)),
+            dma((2 * count,)),
             dma((2 * count,)),
             dma((2 * sides,)),
-            dma((1,)),
+            dma((2,)),
         ],
         compiler_params=pltpu.CompilerParams(
             collective_id=0, has_side_effects=True, vmem_limit_bytes=16 * 2**20
@@ -476,7 +495,7 @@
         out_shape=jax.ShapeDtypeStruct(
             (members * clusters, taps, depth // members, species), weights.dtype
         ),
-        in_specs=[vmem, pl.BlockSpec(memory_space=pl.ANY)],
+        in_specs=[vmem, pl.BlockSpec(memory_space=pltpu.HBM)],
         out_specs=vmem,
         scratch_shapes=[
             pltpu.VMEM((clusters,) + block, weights.dtype),

time: 62.8 us -> 59.2 us (0.943); the launches traced: 62 us -> 59 us
  Pallas kernels: 58 us -> 55 us
    pallas_call x1, Pallas kernels: 18.9 us -> 16.4 us  [group_rows(): pl.pallas_call(functools.partial(gather_kernel, members, groups, sides),...]
    pallas_call x1, Pallas kernels: 27.3 us -> 26 us  [new_shares(): pl.pallas_call(functools.partial(reduce_kernel, members, groups, step), o...]
    pallas_call x1, Pallas kernels: 11.8 us -> 12.6 us  [gradient_shares(): pl.pallas_call(functools.partial(head_kernel, members), out_shape=jax.Sha...]
where the time goes in v5:
time: 59.2 us; the launch traced here: 59 us
  Pallas kernels  55 us (93%)
  local copies, waits for them, and re-layouts  4.01 us (7%)
    pallas_call x1, Pallas kernels, new_shares(): pl.pallas_call(functools.partial(reduce_kernel, members, groups, step), o...  26 us
    pallas_call x1, Pallas kernels, group_rows(): pl.pallas_call(functools.partial(gather_kernel, members, groups, sides),...  16.4 us
    pallas_call x1, Pallas kernels, gradient_shares(): pl.pallas_call(functools.partial(head_kernel, members), out_shape=jax.Sha...  12.6 us
    unnamed x9, local copies, waits for them, and re-layouts  4.01 us

profile of v5, /device:TPU:17, one launch (start us, length us, event | category | flops | bytes accessed | tf_op | source)
XLA Modules:
  0.0 59.0 jit_solution(18446391770991519370)
XLA Ops:
  0.0 0.0 copy-start.1
  0.0 0.9 %copy-done.1 = bf16[8,64,256]{2,1,0:T(8,128)(2,1)S(1)} copy-done((bf16[8,64,256]{2,1,0:T(8,128)(2,1)S(1)}, bf16[8,64,256]{2,1,0:T(8,128)(2,1)}, u32[]{:S(2)}) %copy-start.1) | copy-done | bytes 262168
  1.0 0.0 copy-start.2
  1.0 0.0 copy-start.3
  1.0 16.4 %shard_map.46.map_ref = bf16[34,128,256]{2,1,0:T(8,128)(2,1)S(1)} custom-call(bf16[8,64,256]{2,1,0:T(8,128)(2,1)S(1)} %copy-done.1), custom_call_target="tpu_custom_call" | custom-call | bytes 4000000 | tf_op jit(solution)/shard_map/pallas_call | solution.py:305
  17.4 0.0 copy-done.2
  17.4 0.0 copy-done.3
  17.4 0.0 copy-start
  17.4 2.3 %copy-done = bf16[8,9,256,128]{3,2,1,0:T(8,128)(2,1)S(1)} copy-done((bf16[8,9,256,128]{3,2,1,0:T(8,128)(2,1)S(1)}, bf16[8,9,256,128]{3,2,1,0:T(8,128)(2,1)}, u32[]{:S(2)}) %copy-start) | copy-done | bytes 4718616
  19.7 12.6 %shard_map.47.share_ref = bf16[4,2,9,64,128]{4,3,2,1,0:T(8,128)(2,1)S(1)} custom-call(s32[8,64]{1,0:T(8,128)S(1)} %copy-done.3, bf16[34,128,256]{2,1,0:T(8,128)(2,1)S(1)} %shard_map.46.map_ref, bf16[8,2304,128]{2,1,0:T(8,128)(2,1)S(1)} %bitcast.1, s32[8,64,128]{2,1,0:T(8,128)S(1)} %copy-done.2), custom_call_target="tpu_custom_call" | custom-call | flops 5000000000 | bytes 6000000 | tf_op jit(solution)/shard_map/pallas_call | solution.py:109
  32.4 26.0 %shard_map.48 = bf16[8,9,16,128]{3,2,1,0:T(8,128)(2,1)S(1)} custom-call(bf16[4,2,9,64,128]{4,3,2,1,0:T(8,128)(2,1)S(1)} %shard_map.47.share_ref, bf16[8,9,256,128]{3,2,1,0:T(8,128)(2,1)S(1)} %copy-done), custom_call_target="tpu_custom_call" | custom-call | flops 1000000 | bytes 4000000 | tf_op jit(solution)/shard_map/pallas_call | solution.py:493
  58.3 0.7 %copy.6 = bf16[8,9,16,128]{3,2,1,0:T(8,128)(2,1)} copy(bf16[8,9,16,128]{3,2,1,0:T(8,128)(2,1)S(1)} %shard_map.48) | data formatting | bytes 589824
Async XLA Ops:
  0.0 0.9 %copy-start.1 = (bf16[8,64,256]{2,1,0:T(8,128)(2,1)S(1)}, bf16[8,64,256]{2,1,0:T(8,128)(2,1)}, u32[]{:S(2)}) copy-start(bf16[8,64,256]{2,1,0:T(8,128)(2,1)} %own_ref.1) | copy-start | bytes 786436
  1.0 16.4 %copy-start.2 = (s32[8,64,128]{2,1,0:T(8,128)S(1)}, s32[8,64,128]{2,1,0:T(8,128)}, u32[]{:S(2)}) copy-start(s32[8,64,128]{2,1,0:T(8,128)} %labels_all.1) | copy-start | bytes 786436
  1.0 16.4 %copy-start.3 = (s32[8,64]{1,0:T(8,128)S(1)}, s32[8,64]{1,0:T(8,128)}, u32[]{:S(2)}) copy-start(s32[8,64]{1,0:T(8,128)} %lists_ref.1) | copy-start | bytes 6148
  17.4 2.3 %copy-start = (bf16[8,9,256,128]{3,2,1,0:T(8,128)(2,1)S(1)}, bf16[8,9,256,128]{3,2,1,0:T(8,128)(2,1)}, u32[]{:S(2)}) copy-start(bf16[8,9,256,128]{3,2,1,0:T(8,128)(2,1)} %weights_ref.1) | copy-start | bytes 14155780

commit v6 on v5

--- a/solution.py
+++ b/solution.py
@@ -122,7 +122,7 @@
             pltpu.VMEM((clusters,) + labels.shape[1:], labels.dtype),
             pltpu.SemaphoreType.DMA((2,)),
         ],
-        compiler_params=pltpu.CompilerParams(vmem_limit_bytes=40 * 2**20),
+        compiler_params=pltpu.CompilerParams(vmem_limit_bytes=57 * 2**20),
         cost_estimate=pl.CostEstimate(flops=5 * 10**9, bytes_accessed=6 * 10**6, transcendentals=0),
     )(lists, rows, weights.reshape(count, taps * channels, species), labels)
 
@@ -515,7 +515,7 @@
             dma((clusters + 1,)),
         ],
         compiler_params=pltpu.CompilerParams(
-            collective_id=1, has_side_effects=True, vmem_limit_bytes=24 * 2**20
+            collective_id=1, has_side_effects=True, vmem_limit_bytes=57 * 2**20
         ),
         cost_estimate=pl.CostEstimate(flops=10**6, bytes_accessed=4 * 10**6, transcendentals=0),
     )(share, weights)

time: 59.2 us -> 62.5 us (1.056)
  Pallas kernels: 55 us -> 58.6 us
    pallas_call x1, Pallas kernels: 26 us -> 28.7 us  [new_shares(): pl.pallas_call(functools.partial(reduce_kernel, members, groups, step), o...]
    pallas_call x1, Pallas kernels: 12.6 us -> 13.5 us  [gradient_shares(): pl.pallas_call(functools.partial(head_kernel, members), out_shape=jax.Sha...]
    unnamed x9 -> x5, local copies, waits for them, and re-layouts: 4.01 us -> 4.02 us
where the time goes in v6:
time: 62.5 us; the launch traced here: 62.7 us
  Pallas kernels  58.6 us (94%)
  local copies, waits for them, and re-layouts  4.02 us (6%)
    pallas_call x1, Pallas kernels, new_shares(): pl.pallas_call(functools.partial(reduce_kernel, members, groups, step), o...  28.7 us
    pallas_call x1, Pallas kernels, group_rows(): pl.pallas_call(functools.partial(gather_kernel, members, groups, sides),...  16.4 us
    pallas_call x1, Pallas kernels, gradient_shares(): pl.pallas_call(functools.partial(head_kernel, members), out_shape=jax.Sha...  13.5 us
    unnamed x5, local copies, waits for them, and re-layouts  4.02 us

profile of v6, /device:TPU:17, one launch (start us, length us, event | category | flops | bytes accessed | tf_op | source)
XLA Modules:
  0.0 62.7 jit_solution(17735070863764311778)
XLA Ops:
  0.0 0.0 copy-start.1
  0.0 0.9 %copy-done.1 = bf16[8,64,256]{2,1,0:T(8,128)(2,1)S(1)} copy-done((bf16[8,64,256]{2,1,0:T(8,128)(2,1)S(1)}, bf16[8,64,256]{2,1,0:T(8,128)(2,1)}, u32[]{:S(2)}) %copy-start.1) | copy-done | bytes 262168
  1.0 16.4 %shard_map.46.map_ref = bf16[34,128,256]{2,1,0:T(8,128)(2,1)S(1)} custom-call(bf16[8,64,256]{2,1,0:T(8,128)(2,1)S(1)} %copy-done.1), custom_call_target="tpu_custom_call" | custom-call | bytes 4000000 | tf_op jit(solution)/shard_map/pallas_call | solution.py:305
  17.4 0.0 copy-start
  17.4 1.4 %copy-done = bf16[34,128,256]{2,1,0:T(8,128)(2,1)} copy-done((bf16[34,128,256]{2,1,0:T(8,128)(2,1)}, bf16[34,128,256]{2,1,0:T(8,128)(2,1)S(1)}, u32[]{:S(2)}) %copy-start) | copy-done | bytes 2228248
  18.7 13.5 %shard_map.47.share_ref = bf16[4,2,9,64,128]{4,3,2,1,0:T(8,128)(2,1)} custom-call(s32[8,64]{1,0:T(8,128)} %lists_ref.1, bf16[34,128,256]{2,1,0:T(8,128)(2,1)} %copy-done, bf16[8,2304,128]{2,1,0:T(8,128)(2,1)} %bitcast.1, s32[8,64,128]{2,1,0:T(8,128)} %labels_all.1), custom_call_target="tpu_custom_call" | custom-call | flops 5000000000 | bytes 6000000 | tf_op jit(solution)/shard_map/pallas_call | solution.py:109
  32.2 28.7 %shard_map.48 = bf16[8,9,16,128]{3,2,1,0:T(8,128)(2,1)} custom-call(bf16[4,2,9,64,128]{4,3,2,1,0:T(8,128)(2,1)} %shard_map.47.share_ref, bf16[8,9,256,128]{3,2,1,0:T(8,128)(2,1)} %weights_ref.1), custom_call_target="tpu_custom_call" | custom-call | flops 1000000 | bytes 4000000 | tf_op jit(solution)/shard_map/pallas_call | solution.py:493
  61.0 1.7 %copy.6 = bf16[8,9,16,128]{3,2,1,0:T(8,128)(2,1)} copy(bf16[8,9,16,128]{3,2,1,0:T(8,128)(2,1)} %shard_map.48) | data formatting | bytes 589824
Async XLA Ops:
  0.0 0.9 %copy-start.1 = (bf16[8,64,256]{2,1,0:T(8,128)(2,1)S(1)}, bf16[8,64,256]{2,1,0:T(8,128)(2,1)}, u32[]{:S(2)}) copy-start(bf16[8,64,256]{2,1,0:T(8,128)(2,1)} %own_ref.1) | copy-start | bytes 786436
  17.4 1.4 %copy-start = (bf16[34,128,256]{2,1,0:T(8,128)(2,1)}, bf16[34,128,256]{2,1,0:T(8,128)(2,1)S(1)}, u32[]{:S(2)}) copy-start(bf16[34,128,256]{2,1,0:T(8,128)(2,1)S(1)} %shard_map.46.map_ref) | copy-start | bytes 6684676

commit v7 on v5

--- a/solution.py
+++ b/solution.py
@@ -319,7 +319,7 @@
         compiler_params=pltpu.CompilerParams(
             collective_id=0, has_side_effects=True, vmem_limit_bytes=16 * 2**20
         ),
-        cost_estimate=pl.CostEstimate(flops=0, bytes_accessed=4 * 10**6, transcendentals=0),
+        cost_estimate=pl.CostEstimate(flops=0, bytes_accessed=55 * 10**6, transcendentals=0),
     )(features)
 
 

time: 59.2 us -> 58.2 us (0.983); the launches traced: 59 us -> 57.3 us
  Pallas kernels: 55 us -> 53.3 us
    pallas_call x1, Pallas kernels: 26 us -> 25.1 us  [new_shares(): pl.pallas_call(functools.partial(reduce_kernel, members, groups, step), o...]
    pallas_call x1, Pallas kernels: 12.6 us -> 11.8 us  [gradient_shares(): pl.pallas_call(functools.partial(head_kernel, members), out_shape=jax.Sha...]
where the time goes in v7:
time: 58.2 us; the launch traced here: 57.3 us
  Pallas kernels  53.3 us (92%)
  local copies, waits for them, and re-layouts  4.01 us (7%)
    pallas_call x1, Pallas kernels, new_shares(): pl.pallas_call(functools.partial(reduce_kernel, members, groups, step), o...  25.1 us
    pallas_call x1, Pallas kernels, group_rows(): pl.pallas_call(functools.partial(gather_kernel, members, groups, sides),...  16.4 us
    pallas_call x1, Pallas kernels, gradient_shares(): pl.pallas_call(functools.partial(head_kernel, members), out_shape=jax.Sha...  11.8 us
    unnamed x9, local copies, waits for them, and re-layouts  4.01 us

profile of v7, /device:TPU:17, one launch (start us, length us, event | category | flops | bytes accessed | tf_op | source)
XLA Modules:
  0.0 57.3 jit_solution(18446391770991519370)
XLA Ops:
  0.0 0.0 copy-start.1
  0.0 0.9 %copy-done.1 = bf16[8,64,256]{2,1,0:T(8,128)(2,1)S(1)} copy-done((bf16[8,64,256]{2,1,0:T(8,128)(2,1)S(1)}, bf16[8,64,256]{2,1,0:T(8,128)(2,1)}, u32[]{:S(2)}) %copy-start.1) | copy-done | bytes 262168
  1.0 0.0 copy-start.2
  1.0 0.0 copy-start.3
  1.0 16.4 %shard_map.46.map_ref = bf16[34,128,256]{2,1,0:T(8,128)(2,1)S(1)} custom-call(bf16[8,64,256]{2,1,0:T(8,128)(2,1)S(1)} %copy-done.1), custom_call_target="tpu_custom_call" | custom-call | bytes 55000000 | tf_op jit(solution)/shard_map/pallas_call | solution.py:305
  17.4 0.0 copy-done.2
  17.4 0.0 copy-done.3
  17.4 0.0 copy-start
  17.4 2.3 %copy-done = bf16[8,9,256,128]{3,2,1,0:T(8,128)(2,1)S(1)} copy-done((bf16[8,9,256,128]{3,2,1,0:T(8,128)(2,1)S(1)}, bf16[8,9,256,128]{3,2,1,0:T(8,128)(2,1)}, u32[]{:S(2)}) %copy-start) | copy-done | bytes 4718616
  19.7 11.8 %shard_map.47.share_ref = bf16[4,2,9,64,128]{4,3,2,1,0:T(8,128)(2,1)S(1)} custom-call(s32[8,64]{1,0:T(8,128)S(1)} %copy-done.3, bf16[34,128,256]{2,1,0:T(8,128)(2,1)S(1)} %shard_map.46.map_ref, bf16[8,2304,128]{2,1,0:T(8,128)(2,1)S(1)} %bitcast.1, s32[8,64,128]{2,1,0:T(8,128)S(1)} %copy-done.2), custom_call_target="tpu_custom_call" | custom-call | flops 5000000000 | bytes 6000000 | tf_op jit(solution)/shard_map/pallas_call | solution.py:109
  31.5 25.1 %shard_map.48 = bf16[8,9,16,128]{3,2,1,0:T(8,128)(2,1)S(1)} custom-call(bf16[4,2,9,64,128]{4,3,2,1,0:T(8,128)(2,1)S(1)} %shard_map.47.share_ref, bf16[8,9,256,128]{3,2,1,0:T(8,128)(2,1)S(1)} %copy-done), custom_call_target="tpu_custom_call" | custom-call | flops 1000000 | bytes 4000000 | tf_op jit(solution)/shard_map/pallas_call | solution.py:493
  56.6 0.7 %copy.6 = bf16[8,9,16,128]{3,2,1,0:T(8,128)(2,1)} copy(bf16[8,9,16,128]{3,2,1,0:T(8,128)(2,1)S(1)} %shard_map.48) | data formatting | bytes 589824
Async XLA Ops:
  0.0 0.9 %copy-start.1 = (bf16[8,64,256]{2,1,0:T(8,128)(2,1)S(1)}, bf16[8,64,256]{2,1,0:T(8,128)(2,1)}, u32[]{:S(2)}) copy-start(bf16[8,64,256]{2,1,0:T(8,128)(2,1)} %own_ref.1) | copy-start | bytes 786436
  1.0 16.4 %copy-start.2 = (s32[8,64,128]{2,1,0:T(8,128)S(1)}, s32[8,64,128]{2,1,0:T(8,128)}, u32[]{:S(2)}) copy-start(s32[8,64,128]{2,1,0:T(8,128)} %labels_all.1) | copy-start | bytes 786436
  1.0 16.4 %copy-start.3 = (s32[8,64]{1,0:T(8,128)S(1)}, s32[8,64]{1,0:T(8,128)}, u32[]{:S(2)}) copy-start(s32[8,64]{1,0:T(8,128)} %lists_ref.1) | copy-start | bytes 6148
  17.4 2.3 %copy-start = (bf16[8,9,256,128]{3,2,1,0:T(8,128)(2,1)S(1)}, bf16[8,9,256,128]{3,2,1,0:T(8,128)(2,1)}, u32[]{:S(2)}) copy-start(bf16[8,9,256,128]{3,2,1,0:T(8,128)(2,1)} %weights_ref.1) | copy-start | bytes 14155780
